TPU v7x, 32 devices: a whole 2x2x4 slice. The times are simulated.
32 devices in a mesh: group: 2 (over x), region: 8 (over z, y), sub: 2 (over core).
Axes of the slice: x: 2, y: 2, z: 4, core: 2. Of those that a mesh axis runs over, the one named last changes fastest.
Arguments:
- node_latent: bfloat16 [6144, 512], P(('group', 'region', 'sub')), parts along dimension 0, may hold values from -6 to 6
- edge_latent: bfloat16 [49152, 512], P(('group', 'region', 'sub')), parts along dimension 0, may hold values from -6 to 6
- node_cot: bfloat16 [6144, 512], P(('group', 'region', 'sub')), parts along dimension 0, may hold values from -6 to 6
- edge_cot: bfloat16 [49152, 512], P(('group', 'region', 'sub')), parts along dimension 0, may hold values from -6 to 6
- send_rows: int32 [32, 16, 8], P(('group', 'region', 'sub')), parts along dimension 0, may hold values from 0 to 191, as said below
- edge_sender: int32 [49152], P(('group', 'region', 'sub')), parts along dimension 0, may hold values from 0 to 319, as said below
- edge_receiver: int32 [49152], P(('group', 'region', 'sub')), parts along dimension 0, may hold values from 0 to 191
- edge_first: bfloat16 [1536, 512], replicated, may hold values from -0.15625 to 0.15625
- edge_second: bfloat16 [512, 512], replicated, may hold values from -0.25 to 0.25
- edge_bias: float32 [512], replicated, may hold values from -3 to 3
- edge_gain: float32 [512], replicated, may hold values from 0.5 to 1.5
- edge_shift: float32 [512], replicated, may hold values from -3 to 3
- node_first: bfloat16 [1024, 512], replicated, may hold values from -0.1875 to 0.1875
- node_second: bfloat16 [512, 512], replicated, may hold values from -0.25 to 0.25
- node_bias: float32 [512], replicated, may hold values from -3 to 3
- node_gain: float32 [512], replicated, may hold values from 0.5 to 1.5
Outputs:
- node_grad: bfloat16 [6144, 512], P(('group', 'region', 'sub')), parts along dimension 0
- edge_grad: bfloat16 [49152, 512], P(('group', 'region', 'sub')), parts along dimension 0
- edge_first_grad: float32 [3072, 512], P(('group', 'region', 'sub')), parts along dimension 0
- edge_second_grad: float32 [1024, 512], P(('group', 'region', 'sub')), parts along dimension 0
- edge_vector_grad: float32 [6, 512], P('group', ('region', 'sub')), parts along dimension 0
- node_first_grad: float32 [2048, 512], P(('group', 'region', 'sub')), parts along dimension 0
- node_second_grad: float32 [1024, 512], P(('group', 'region', 'sub')), parts along dimension 0
- node_vector_grad: float32 [4, 512], P('group', ('region', 'sub')), parts along dimension 0
There are 2 independent parts, one for each index of `group`. A program takes and returns all parts, laid end to end along the dimension named above; an argument that names none is the same for every part. Nothing has to cross between parts.
Inputs may be any that keep to these rules, and one draw needn't show every extreme that they name: `send_rows`: own nodes of the sending device. `edge_sender`: within each device's 1536 edges the entries ascend. An entry below 192 is an own node; an entry v at or above it is slot (v - 192) % 8 of the halo that device (v - 192) // 8 sends to this device. Some slots are named by no edge.
All inputs are finite; a program needn't handle non-finite values.
Results may differ from a plain program's by a relative error of at most 0.012.
Values may be sent and summed in bfloat16 or wider, within the bound.
A program may use at most 128 MiB of HBM per device.

v0:
```python
import math

import jax
import jax.numpy as jnp
from jax import lax
from jax.sharding import PartitionSpec as P


def mlp_forward(inputs, first, bias, second):
    before = jnp.dot(inputs, first, preferred_element_type=jnp.float32) + bias
    active = jax.nn.silu(before).astype(jnp.bfloat16)
    output = jnp.dot(active, second, preferred_element_type=jnp.float32)
    centred = output - jnp.mean(output, axis=-1, keepdims=True)
    inverse = lax.rsqrt(jnp.mean(centred * centred, axis=-1, keepdims=True) + 1e-05)
    return (before, active, centred * inverse, inverse)


def mlp_backward(inputs, first, second, gain, before, active, normed, inverse, upstream):
    grad_norm = upstream * gain
    centred = grad_norm - jnp.mean(grad_norm, axis=-1, keepdims=True)
    grad_out = (
        inverse * (centred - normed * jnp.mean(grad_norm * normed, axis=-1, keepdims=True))
    ).astype(jnp.bfloat16)
    sigmoid = jax.nn.sigmoid(before)
    grad_before = jnp.dot(grad_out, second.T, preferred_element_type=jnp.float32) * (
        sigmoid + before * sigmoid * (1.0 - sigmoid)
    )
    grad_pre = grad_before.astype(jnp.bfloat16)
    grad_inputs = jnp.dot(grad_pre, first.T, preferred_element_type=jnp.float32)
    grad_first = jnp.dot(inputs.T, grad_pre, preferred_element_type=jnp.float32)
    grad_second = jnp.dot(active.T, grad_out, preferred_element_type=jnp.float32)
    return (
        grad_inputs,
        grad_first,
        grad_second,
        jnp.sum(grad_before, axis=0),
        jnp.sum(upstream * normed, axis=0),
    )


def on_device(
    node_latent,
    edge_latent,
    node_cot,
    edge_cot,
    send_rows,
    edge_sender,
    edge_receiver,
    edge_first,
    edge_second,
    edge_bias,
    edge_gain,
    edge_shift,
    node_first,
    node_second,
    node_bias,
    node_gain,
):
    peers = lax.axis_size(("region", "sub"))
    node_rows, latent = node_latent.shape
    send_table = send_rows.reshape(peers, -1)
    slots_each = send_table.shape[1]
    outgoing = node_latent[send_table]
    arrived = lax.all_to_all(outgoing, ("region", "sub"), split_axis=0, concat_axis=0, tiled=True)
    halo_table = jnp.concatenate([node_latent, arrived.reshape(peers * slots_each, latent)], axis=0)
    edge_input = jnp.concatenate(
        [edge_latent, halo_table[edge_sender], node_latent[edge_receiver]], axis=1
    )
    e_before, e_active, e_normed, e_inverse = mlp_forward(
        edge_input, edge_first, edge_bias, edge_second
    )
    message = (e_normed * edge_gain + edge_shift).astype(jnp.bfloat16)
    aggregate = jax.ops.segment_sum(
        message.astype(jnp.float32), edge_receiver, num_segments=node_rows
    ).astype(jnp.bfloat16)
    node_input = jnp.concatenate([node_latent, aggregate], axis=1)
    n_before, n_active, n_normed, n_inverse = mlp_forward(
        node_input, node_first, node_bias, node_second
    )
    node_upstream = node_cot.astype(jnp.float32)
    n_input_grad, n_first_grad, n_second_grad, n_bias_grad, n_gain_grad = mlp_backward(
        node_input,
        node_first,
        node_second,
        node_gain,
        n_before,
        n_active,
        n_normed,
        n_inverse,
        node_upstream,
    )
    message_grad = edge_cot.astype(jnp.float32) + n_input_grad[:, latent:][edge_receiver]
    e_input_grad, e_first_grad, e_second_grad, e_bias_grad, e_gain_grad = mlp_backward(
        edge_input,
        edge_first,
        edge_second,
        edge_gain,
        e_before,
        e_active,
        e_normed,
        e_inverse,
        message_grad,
    )
    edge_grad = (edge_cot.astype(jnp.float32) + e_input_grad[:, :latent]).astype(jnp.bfloat16)
    sender_grads = jax.ops.segment_sum(
        e_input_grad[:, latent : 2 * latent],
        edge_sender,
        num_segments=node_rows + peers * slots_each,
    )
    halo_back = sender_grads[node_rows:].reshape(peers, slots_each, latent)
    returned = lax.all_to_all(
        halo_back.astype(jnp.bfloat16), ("region", "sub"), split_axis=0, concat_axis=0, tiled=True
    ).astype(halo_back.dtype)
    node_total = node_upstream + n_input_grad[:, :latent] + sender_grads[:node_rows]
    node_total = node_total + jax.ops.segment_sum(
        e_input_grad[:, 2 * latent :], edge_receiver, num_segments=node_rows
    )
    node_total = node_total + jax.ops.segment_sum(
        returned.reshape(peers * slots_each, latent), send_table.reshape(-1), num_segments=node_rows
    )
    edge_scale = 1.0 / math.sqrt(edge_latent.shape[0] * peers)
    node_scale = 1.0 / math.sqrt(node_rows * peers)
    edge_vectors = jnp.stack([e_bias_grad, e_gain_grad, jnp.sum(message_grad, axis=0)]) * edge_scale
    node_vectors = jnp.stack([n_bias_grad, n_gain_grad]) * node_scale
    partials = (
        e_first_grad * edge_scale,
        e_second_grad * edge_scale,
        edge_vectors,
        n_first_grad * node_scale,
        n_second_grad * node_scale,
        node_vectors,
    )
    summed = (
        lax.psum_scatter(partials[0], ("region", "sub"), scatter_dimension=0, tiled=True),
        lax.psum_scatter(partials[1], ("region", "sub"), scatter_dimension=0, tiled=True),
        lax.psum_scatter(partials[2], ("region", "sub"), scatter_dimension=1, tiled=True),
        lax.psum_scatter(partials[3], ("region", "sub"), scatter_dimension=0, tiled=True),
        lax.psum_scatter(partials[4], ("region", "sub"), scatter_dimension=0, tiled=True),
        lax.psum_scatter(partials[5], ("region", "sub"), scatter_dimension=1, tiled=True),
    )
    return (
        node_total.astype(jnp.bfloat16),
        edge_grad,
        summed[0],
        summed[1],
        summed[2],
        summed[3],
        summed[4],
        summed[5],
    )


def solution(mesh):
    placed = (
        P(("group", "region", "sub"), None),
        P(("group", "region", "sub"), None),
        P(("group", "region", "sub"), None),
        P(("group", "region", "sub"), None),
        P(("group", "region", "sub"), None, None),
        P(("group", "region", "sub")),
        P(("group", "region", "sub")),
        P(),
        P(),
        P(),
        P(),
        P(),
        P(),
        P(),
        P(),
        P(),
    )
    return jax.shard_map(
        on_device,
        mesh=mesh,
        in_specs=placed,
        out_specs=(
            P(("group", "region", "sub"), None),
            P(("group", "region", "sub"), None),
            P(("group", "region", "sub"), None),
            P(("group", "region", "sub"), None),
            P("group", ("region", "sub")),
            P(("group", "region", "sub"), None),
            P(("group", "region", "sub"), None),
            P("group", ("region", "sub")),
        ),
        check_vma=False,
    )
```

profile of v0, /device:TPU:0, one launch (start us, length us, event | category | flops | bytes accessed | tf_op | source)
XLA Modules:
  0.0 465.1 jit_solution(13513281999682540658)
XLA Ops:
  8.2 2.5 gather_fusion
  10.7 7.4 %all-to-all-start = ((bf16[16,8,512]{2,1,0:T(8,128)(2,1)}), bf16[16,8,512]{2,1,0:T(8,128)(2,1)S(1)}, u32[]{:S(2)}, u32[]{:S(2)}) async-start(bf16[16,8,512]{2,1,0:T(8,128)(2,1)} %bitcast.1), calls=%async_computation | async-start | bytes 262144 | tf_op jit(solution)/shard_map/all_to_all | solution.py:64
  18.9 5.4 %gather_fusion.2 = bf16[1536,512]{1,0:T(8,128)(2,1)} fusion(bf16[192,512]{1,0:T(8,128)(2,1)S(1)} %copy-done.1, s32[2048]{0:T(1024)S(1)} %pad_clamp_fusion), kind=kCustom, calls=%fused_computation.2 | custom fusion | bytes 3151872 | tf_op jit(solution)/shard_map/gather | solution.py:67
  25.9 2.7 constant_dynamic-update-slice_fusion.2
  28.6 5.4 %gather_fusion.1 = bf16[1536,512]{1,0:T(8,128)(2,1)} fusion(bf16[320,512]{1,0:T(8,128)(2,1)S(1)} %pad_maximum_fusion.1, s32[2048]{0:T(1024)S(1)} %pad_clamp_fusion.1), kind=kCustom, calls=%fused_computation.1 | custom fusion | bytes 3151872 | tf_op jit(solution)/shard_map/gather | solution.py:67
  34.1 2.8 constant_dynamic-update-slice_fusion.1
  38.2 7.1 %fusion.6 = (bf16[1536,512]{1,0:T(8,128)(2,1)S(1)}, f32[1536,512]{1,0:T(8,128)}) fusion(f32[512]{0:T(512)S(1)} %copy-done.38, bf16[1536,1536]{1,0:T(8,128)(2,1)} %constant_dynamic-update-slice_fusion, bf16[1536,512]{1,0:T(8,128)(2,1)S(1)} %copy-done), kind=kOutput, calls=%fused_computation.27 | convolution fusion | flops 2420637696 | bytes 11012096 | tf_op jit(solution)/shard_map/dot_general | solution.py:10
  48.2 2.3 fusion.7
  50.4 3.6 copy.38
  54.0 10.6 %scatter_custom_fusion = f32[192,512]{1,0:T(8,128)S(1)} fusion(s32[1536]{0:T(1024)} %param.22, f32[1536,512]{1,0:T(8,128)} %copy.38, f32[]{:T(128)} %constant.10.clone.1), kind=kCustom, calls=%fused_computation.62 | custom fusion | flops 786432 | bytes 393728 | tf_op jit(solution)/shard_map/scatter-add | solution.py:73
  70.4 4.9 %gather_fusion.3 = f32[1536,512]{1,0:T(8,128)} fusion(f32[192,512]{1,0:T(8,128)S(1)} %slice.38, s32[2048]{0:T(1024)S(1)} %copy-done.21), kind=kCustom, calls=%fused_computation.3 | custom fusion | bytes 6297600 | tf_op jit(solution)/shard_map/gather | solution.py:92
  75.3 3.8 copy.40
  79.1 4.8 %multiply_reduce_fusion = (f32[512]{0:T(512)}, f32[1536]{0:T(1024)S(1)}, f32[1536]{0:T(1024)S(1)}, f32[512]{0:T(512)}) fusion(f32[1536,512]{0,1:T(8,128)} %copy-done.2, f32[1536]{0:T(1024)S(1)} %add_rsqrt_fusion, f32[1536]{0:T(1024)S(1)} %broadcast_multiply_fusion.2, f32[1536,512]{0,1:T(8,128)} %copy.40, bf16[1536,512]{0,1:T(8,128)(2,1)S(1)} %copy-done.3, ...), kind=kLoop, calls=%fused_computation.18 | loop fusion | flops 8646656 | bytes 7895040 | tf_op jit(solution)/shard_map/reduce_sum | solution.py:37
  87.4 4.2 multiply_convert_fusion
  91.6 3.1 fusion.43
  95.7 2.6 convolution_multiply_fusion.4
  98.4 3.9 convolution_multiply_fusion.3
  102.4 2.8 convolution_multiply_fusion.2
  105.5 7.2 %convolution_multiply_fusion = f32[1536,512]{1,0:T(8,128)} fusion(bf16[1536,1536]{1,0:T(8,128)(2,1)} %constant_dynamic-update-slice_fusion, bf16[1536,512]{1,0:T(8,128)(2,1)} %get-tuple-element.46), kind=kOutput, calls=%fused_computation.10 | convolution fusion | flops 2416705536 | bytes 9437184 | tf_op jit(solution)/shard_map/dot_general | solution.py:30
  113.5 4.1 fusion.9
  117.6 3.6 copy-done.4
  123.1 11.8 %scatter_custom_fusion.1 = f32[320,512]{1,0:T(8,128)} fusion(s32[1536]{0:T(1024)} %param.21, f32[1536,1536]{1,0:T(8,128)} %copy-done.4, f32[]{:T(128)} %constant.10.clone.1), kind=kCustom, calls=%fused_computation.16 | custom fusion | flops 786432 | bytes 3801600 | tf_op jit(solution)/shard_map/scatter-add | solution.py:105
  134.9 3.5 copy.48
  138.5 3.6 fusion
  142.0 2.7 copy.43
  145.4 6.1 %all-to-all-start.1 = ((bf16[16,8,512]{2,1,0:T(8,128)(2,1)}), bf16[16,8,512]{2,1,0:T(8,128)(2,1)S(1)}, u32[]{:S(2)}, u32[]{:S(2)}) async-start(bf16[16,8,512]{2,1,0:T(8,128)(2,1)} %fusion.28), calls=%async_computation.1 | async-start | bytes 262144 | tf_op jit(solution)/shard_map/all_to_all | solution.py:111
  152.4 12.2 %scatter_custom_fusion.2 = f32[192,512]{1,0:T(8,128)} fusion(f32[192,512]{1,0:T(8,128)} %fusion.18, s32[1536]{0:T(1024)} %param.22, f32[1536,1536]{1,0:T(8,128)} %copy-done.4), kind=kCustom, calls=%fused_computation.14 | custom fusion | flops 786432 | bytes 3538944 | tf_op jit(solution)/shard_map/scatter-add | solution.py:115
  165.9 36.1 %reduce-scatter.19.cloned.1.call-done = f32[32,3]{1,0:T(8,128)} async-done(((f32[512,3]{1,0:T(8,128)}), f32[32,3]{1,0:T(8,128)}) %reduce-scatter.19.cloned.1.call-update) | async-done | bytes 400
  206.5 56.1 %reduce-scatter.17.cloned.1.call-done = f32[32,512]{1,0:T(8,128)} async-done(((f32[512,512]{1,0:T(8,128)}), f32[32,512]{1,0:T(8,128)}) %reduce-scatter.17.cloned.1.call-update) | async-done | bytes 65552 | tf_op jit(solution)/shard_map/reduce_scatter | solution.py:138
  262.6 61.0 %reduce-scatter.13.cloned.1.call-done = f32[32,512]{1,0:T(8,128)} async-done(((f32[512,512]{1,0:T(8,128)}), f32[32,512]{1,0:T(8,128)}) %reduce-scatter.13.cloned.1.call-update) | async-done | bytes 65552 | tf_op jit(solution)/shard_map/reduce_scatter | solution.py:135
  323.6 64.7 %reduce-scatter.15.cloned.1.call-done = f32[64,512]{1,0:T(8,128)} async-done(((f32[1024,512]{1,0:T(8,128)}), f32[64,512]{1,0:T(8,128)}) %reduce-scatter.15.cloned.1.call-update) | async-done | bytes 131088 | tf_op jit(solution)/shard_map/reduce_scatter | solution.py:137
  388.3 70.0 %reduce-scatter.11.cloned.1.call-done = f32[96,512]{1,0:T(8,128)} async-done(((f32[1536,512]{1,0:T(8,128)}), f32[96,512]{1,0:T(8,128)}) %reduce-scatter.11.cloned.1.call-update) | async-done | bytes 196624 | tf_op jit(solution)/shard_map/reduce_scatter | solution.py:134
  (139 shorter events, 28.2 us)
Async XLA Ops:
  7.2 31.0 %copy-start = (bf16[1536,512]{1,0:T(8,128)(2,1)S(1)}, bf16[1536,512]{1,0:T(8,128)(2,1)}, u32[]{:S(2)}) copy-start(bf16[1536,512]{1,0:T(8,128)(2,1)} %param.23) | copy-start | bytes 4718596
  7.2 11.7 %copy-start.1 = (bf16[192,512]{1,0:T(8,128)(2,1)S(1)}, bf16[192,512]{1,0:T(8,128)(2,1)}, u32[]{:S(2)}) copy-start(bf16[192,512]{1,0:T(8,128)(2,1)} %param.16) | copy-start | bytes 589828
  10.7 17.9 %all-to-all-start = ((bf16[16,8,512]{2,1,0:T(8,128)(2,1)}), bf16[16,8,512]{2,1,0:T(8,128)(2,1)S(1)}, u32[]{:S(2)}, u32[]{:S(2)}) async-start(bf16[16,8,512]{2,1,0:T(8,128)(2,1)} %bitcast.1), calls=%async_computation | async-start | bytes 262144 | tf_op jit(solution)/shard_map/all_to_all | solution.py:64
  18.1 146.4 %reduce-scatter.21.cloned.1.call-start = ((), (), s32[]{:S(2)}) async-start(), calls=%async_computation.13 | async-start | bytes 278528
  18.8 5.5 %copy-start.20 = (s32[2048]{0:T(1024)}, s32[2048]{0:T(1024)S(1)}, u32[]{:S(2)}) copy-start(s32[2048]{0:T(1024)S(1)} %pad_clamp_fusion) | copy-start | bytes 24580
  18.9 5.5 %copy-start.27 = (s32[1536]{0:T(1024)S(1)}, s32[1536]{0:T(1024)}, u32[]{:S(2)}) copy-start(s32[1536]{0:T(1024)} %param.21) | copy-start | bytes 18436
  18.9 5.5 %copy-start.10 = (bf16[1536,512]{1,0:T(8,128)(2,1)S(1)}, bf16[1536,512]{1,0:T(8,128)(2,1)}, u32[]{:S(2)}) copy-start(bf16[1536,512]{1,0:T(8,128)(2,1)} %param.19) | copy-start | bytes 4718596
  34.1 4.1 copy-start.38
  38.2 7.1 %copy-start.18 = (bf16[512,512]{1,0:T(8,128)(2,1)S(1)}, bf16[512,512]{1,0:T(8,128)(2,1)}, u32[]{:S(2)}) copy-start(bf16[512,512]{1,0:T(8,128)(2,1)} %param.24) | copy-start | bytes 1572868
  50.4 14.2 %copy-start.13 = (bf16[1024,512]{1,0:T(8,128)(2,1)S(1)}, bf16[1024,512]{1,0:T(8,128)(2,1)}, u32[]{:S(2)}) copy-start(bf16[1024,512]{1,0:T(8,128)(2,1)} %param.28) | copy-start | bytes 3145732
  50.4 14.2 %copy-start.39 = (f32[512]{0:T(512)S(1)}, f32[512]{0:T(512)}, u32[]{:S(2)}) copy-start(f32[512]{0:T(512)} %param.30) | copy-start | bytes 6148
  54.0 13.2 %copy-start.15 = (bf16[192,512]{1,0:T(8,128)(2,1)S(1)}, bf16[192,512]{1,0:T(8,128)(2,1)}, u32[]{:S(2)}) copy-start(bf16[192,512]{1,0:T(8,128)(2,1)} %param.18) | copy-start | bytes 589828
  54.0 13.2 %copy-start.33 = (f32[512]{0:T(512)S(1)}, f32[512]{0:T(512)}, u32[]{:S(2)}) copy-start(f32[512]{0:T(512)} %param.31) | copy-start | bytes 6148
  64.6 3.4 copy-start.37
  65.4 3.7 copy-start.40
  65.4 3.7 copy-start.14
  75.3 3.8 copy-start.3
  79.1 6.0 %copy-start.26 = (f32[512]{0:T(512)S(1)}, f32[512]{0:T(512)}, u32[]{:S(2)}) copy-start(f32[512]{0:T(512)} %get-tuple-element.36) | copy-start | bytes 6148
  79.1 6.1 %copy-start.34 = (f32[512]{0:T(512)S(1)}, f32[512]{0:T(512)}, u32[]{:S(2)}) copy-start(f32[512]{0:T(512)} %get-tuple-element.47) | copy-start | bytes 6148
  87.3 114.7 %reduce-scatter.19.cloned.1.call-start = ((), (), s32[]{:S(2)}) async-start(), calls=%async_computation.12 | async-start | bytes 278528
  87.4 4.2 copy-start.19
  87.4 4.2 copy-start.41
  91.6 3.2 copy-start.12
  91.6 4.1 copy-start.25
  91.6 4.1 copy-start.31
  95.7 167.0 %reduce-scatter.17.cloned.1.call-start = ((), (), s32[]{:S(2)}) async-start(), calls=%async_computation.11 | async-start | bytes 1114112 | tf_op jit(solution)/shard_map/reduce_scatter | solution.py:138
  98.4 225.2 %reduce-scatter.13.cloned.1.call-start = ((), (), s32[]{:S(2)}) async-start(), calls=%async_computation.9 | async-start | bytes 1114112 | tf_op jit(solution)/shard_map/reduce_scatter | solution.py:135
  102.4 285.9 %reduce-scatter.15.cloned.1.call-start = ((), (), s32[]{:S(2)}) async-start(), calls=%async_computation.10 | async-start | bytes 2228224 | tf_op jit(solution)/shard_map/reduce_scatter | solution.py:137
  105.2 353.0 %reduce-scatter.11.cloned.1.call-start = ((), (), s32[]{:S(2)}) async-start(), calls=%async_computation.8 | async-start | bytes 3342336 | tf_op jit(solution)/shard_map/reduce_scatter | solution.py:134
  117.6 3.6 copy-start.4
  142.0 9.5 %copy-start.8 = (f32[192,1024]{1,0:T(8,128)S(1)}, f32[192,1024]{1,0:T(8,128)}, u32[]{:S(2)}) copy-start(f32[192,1024]{1,0:T(8,128)} %copy-done.7) | copy-start | bytes 2359300
  145.4 57.9 %all-to-all-start.1 = ((bf16[16,8,512]{2,1,0:T(8,128)(2,1)}), bf16[16,8,512]{2,1,0:T(8,128)(2,1)S(1)}, u32[]{:S(2)}, u32[]{:S(2)}) async-start(bf16[16,8,512]{2,1,0:T(8,128)(2,1)} %fusion.28), calls=%async_computation.1 | async-start | bytes 262144 | tf_op jit(solution)/shard_map/all_to_all | solution.py:111
  (18 other events, 33.8 us)
Sparse Core Ops, SparseCore 0:
  87.4 56.6 reduce-scatter.20
  147.6 54.3 reduce-scatter.18
  206.2 56.4 reduce-scatter.16
  267.1 56.4 reduce-scatter.12
  327.8 60.4 reduce-scatter.14
  393.0 65.2 reduce-scatter.10
where the time goes:
time: 466 us; the launch traced here: 465 us
  waiting for transfers between devices  288 us (62%)
  other arithmetic  58.2 us (12%)
  local copies, waits for them, and re-layouts  55.3 us (12%)
  matrix products  35.2 us (8%)
  between operations  14.6 us (3%)
  starting transfers between devices  13.9 us (3%)
    reduce_scatter x1, waiting for transfers between devices, on_device(): lax.psum_scatter(partials[0], ('region', 'sub'), scatter_dimension=0, til...  70 us
    reduce_scatter x1, waiting for transfers between devices, on_device(): lax.psum_scatter(partials[3], ('region', 'sub'), scatter_dimension=0, til...  64.7 us
    reduce_scatter x1, waiting for transfers between devices, on_device(): lax.psum_scatter(partials[1], ('region', 'sub'), scatter_dimension=0, til...  61 us
    reduce_scatter x1, waiting for transfers between devices, on_device(): lax.psum_scatter(partials[4], ('region', 'sub'), scatter_dimension=0, til...  56.1 us
    unnamed x8, waiting for transfers between devices  36.2 us
    unnamed x94, local copies, waits for them, and re-layouts  25.5 us
    scatter-add x1, other arithmetic, on_device(): jax.ops.segment_sum(e_input_grad[:, 2 * latent:], edge_receiver, num_segm...  12.2 us
    scatter-add x1, other arithmetic, on_device(): jax.ops.segment_sum(e_input_grad[:, latent:2 * latent], edge_sender, num_...  11.8 us
  transfers between devices with their start and end apart: 8, of which 5 were waited for; matrix products, arithmetic and copies ran while one was open for 18% of the time, Pallas kernels for 0%

commit v1 on v0

v1 whole, which is shorter than its diff:
```python
import functools
import math

import jax
import jax.numpy as jnp
from jax import lax
from jax.experimental import pallas as pl
from jax.experimental.pallas import tpu as pltpu
from jax.sharding import PartitionSpec as P

MESH = pl.DeviceIdType.MESH
F32 = jnp.float32
BF16 = jnp.bfloat16
VMEM_LIMIT = 56 * 1024 * 1024


def mm(a, b):
    return jnp.dot(a, b, preferred_element_type=F32)


def mm_nt(a, b):
    return lax.dot_general(a, b, (((1,), (1,)), ((), ())), preferred_element_type=F32)


def mm_tn(a, b):
    return lax.dot_general(a, b, (((0,), (0,)), ((), ())), preferred_element_type=F32)


def one_hot(mask):
    return jnp.where(mask, 1.0, 0.0).astype(BF16)


def fold(x, k):
    if k == 1:
        return x
    w = x.shape[-1] // k
    return jnp.concatenate([x[..., j * w : (j + 1) * w] for j in range(k)], axis=-2)


def unfold(x, k):
    if k == 1:
        return x
    m = x.shape[-2] // k
    return jnp.concatenate([x[..., j * m : (j + 1) * m, :] for j in range(k)], axis=-1)


def place(index, subs):
    return {"region": index // subs, "sub": lax.rem(index, subs)}


def greet_all(me, peers, subs):
    barrier = pltpu.get_barrier_semaphore()

    @pl.loop(1, peers)
    def _(d):
        pl.semaphore_signal(
            barrier, inc=1, device_id=place(lax.rem(me + d, peers), subs), device_id_type=MESH
        )

    return barrier


def halo_kernel(regions, subs, rows_ref, latent_ref, halo_ref, sent, got, send_sem, recv_sem):
    peers = regions * subs
    me = lax.axis_index("region") * subs + lax.axis_index("sub")
    barrier = greet_all(me, peers, subs)
    slots = halo_ref.shape[0] // peers
    nodes, latent = latent_ref.shape
    picked = mm(
        one_hot(lax.broadcasted_iota(jnp.int32, (peers * slots, nodes), 1) == rows_ref[...]),
        latent_ref[...],
    )
    packed = fold(picked.reshape(peers, slots, latent), 2).astype(BF16)
    sent[...] = packed
    pl.semaphore_wait(barrier, peers - 1)

    def copy(d, target, slot):
        return pltpu.make_async_remote_copy(
            src_ref=sent.at[target],
            dst_ref=got.at[slot],
            send_sem=send_sem.at[d],
            recv_sem=recv_sem.at[d],
            device_id=place(target, subs),
            device_id_type=MESH,
        )

    @pl.loop(1, peers)
    def _(d):
        copy(d, lax.rem(me + d, peers), me).start()

    got[me] = sent[me]

    @pl.loop(1, peers)
    def _(d):
        copy(d, lax.rem(me + d, peers), lax.rem(me + peers - d, peers)).wait_recv()

    halo_ref[...] = (
        unfold(got[...].astype(F32), 2).reshape(peers * slots, latent).astype(BF16)
    )

    @pl.loop(1, peers)
    def _(d):
        copy(d, lax.rem(me + d, peers), me).wait_send()


def layer_norm(out):
    centred = out - jnp.mean(out, axis=-1, keepdims=True)
    inverse = lax.rsqrt(jnp.mean(centred * centred, axis=-1, keepdims=True) + 1e-05)
    return centred * inverse, inverse


def norm_backward(upstream, gain, normed, inverse):
    grad_norm = upstream * gain
    centred = grad_norm - jnp.mean(grad_norm, axis=-1, keepdims=True)
    share = jnp.mean(grad_norm * normed, axis=-1, keepdims=True)
    return (inverse * (centred - normed * share)).astype(BF16)


def activate(before):
    s = jax.nn.sigmoid(before)
    return (before * s).astype(BF16), s + before * s * (1.0 - s)


def compute_kernel(
    peers,
    tile,
    nl_ref,
    el_ref,
    nc_ref,
    ec_ref,
    halo_ref,
    cols_ref,
    rows_ref,
    ef_ref,
    es_ref,
    eb_ref,
    eg_ref,
    esh_ref,
    nf_ref,
    ns_ref,
    nb_ref,
    ng_ref,
    edge_out,
    node_part,
    ret_ref,
    gef_ref,
    ges_ref,
    gnf_ref,
    gns_ref,
    hot,
    hot_t,
    table,
    projected,
    active_s,
    dsilu_s,
    normed_s,
    inverse_s,
    agg,
    sums,
    vec,
):
    edges, latent = el_ref.shape
    nodes = nl_ref.shape[0]
    halo = halo_ref.shape[0]
    total = 2 * nodes + halo
    edge_scale = 1.0 / math.sqrt(edges * peers)
    node_scale = 1.0 / math.sqrt(nodes * peers)
    steps = edges // tile
    first = ef_ref.at[pl.ds(0, latent)]
    sender = ef_ref.at[pl.ds(latent, latent)]
    receiver = ef_ref.at[pl.ds(2 * latent, latent)]

    nl = nl_ref[...]
    table[pl.ds(0, nodes), :] = nl
    table[pl.ds(nodes, halo), :] = halo_ref[...]
    projected[pl.ds(0, nodes), :] = mm(nl, receiver[...]).astype(BF16)
    projected[pl.ds(nodes, nodes + halo), :] = mm(table[...], sender[...]).astype(BF16)
    agg[...] = jnp.zeros_like(agg)
    sums[...] = jnp.zeros_like(sums)
    vec[...] = jnp.zeros_like(vec)

    @pl.loop(0, steps)
    def _(t):
        at = pl.ds(pl.multiple_of(t * tile, tile), tile)
        iota = lax.broadcasted_iota(jnp.int32, (tile, total), 1)
        h = one_hot((cols_ref[at, 0:1] == iota) | (cols_ref[at, 1:2] == iota))
        hot[at, :] = h
        iota_t = lax.broadcasted_iota(jnp.int32, (total, tile), 0)
        hot_t[:, at] = one_hot((rows_ref[0:1, at] == iota_t) | (rows_ref[1:2, at] == iota_t))
        before = mm(el_ref[at, :], first[...]) + mm(h, projected[...]) + eb_ref[...]
        active, dsilu = activate(before)
        active_s[at, :] = active
        dsilu_s[at, :] = dsilu
        normed, inverse = layer_norm(mm(active, es_ref[...]))
        normed_s[at, :] = normed
        inverse_s[at, :] = inverse
        message = (normed * eg_ref[...] + esh_ref[...]).astype(BF16)
        agg[...] += mm(hot_t[pl.ds(0, nodes), at], message)

    aggregate = agg[...].astype(BF16)
    top = nf_ref.at[pl.ds(0, latent)]
    low = nf_ref.at[pl.ds(latent, latent)]
    before = mm(nl, top[...]) + mm(aggregate, low[...]) + nb_ref[...]
    active, dsilu = activate(before)
    normed, inverse = layer_norm(mm(active, ns_ref[...]))
    cot = nc_ref[...].astype(F32)
    grad_out = norm_backward(cot, ng_ref[...], normed, inverse)
    grad_before = mm_nt(grad_out, ns_ref[...]) * dsilu
    grad_pre = grad_before.astype(BF16)
    gns_ref[...] = mm_tn(active, grad_out) * node_scale
    gnf_ref[pl.ds(0, latent), :] = mm_tn(nl, grad_pre) * node_scale
    gnf_ref[pl.ds(latent, latent), :] = mm_tn(aggregate, grad_pre) * node_scale
    node_part[...] = cot + mm_nt(grad_pre, top[...])
    spread = mm_nt(grad_pre, low[...]).astype(BF16)
    vec[3:4, :] = jnp.sum(grad_before, axis=0, keepdims=True) * node_scale
    vec[4:5, :] = jnp.sum(cot * normed, axis=0, keepdims=True) * node_scale
    agg[...] = jnp.zeros_like(agg)
    gef_ref[pl.ds(0, latent), :] = jnp.zeros((latent, latent), F32)
    ges_ref[...] = jnp.zeros_like(ges_ref)
    projected[pl.ds(0, nodes), :] = spread

    @pl.loop(0, steps)
    def _(t):
        at = pl.ds(pl.multiple_of(t * tile, tile), tile)
        cot = ec_ref[at, :].astype(F32)
        grad = cot + mm(hot[at, pl.ds(0, nodes)], projected[pl.ds(0, nodes), :])
        normed = normed_s[at, :]
        grad_out = norm_backward(grad, eg_ref[...], normed, inverse_s[at, :])
        grad_before = mm_nt(grad_out, es_ref[...]) * dsilu_s[at, :]
        grad_pre = grad_before.astype(BF16)
        vec[0:1, :] += jnp.sum(grad_before, axis=0, keepdims=True) * edge_scale
        vec[1:2, :] += jnp.sum(grad * normed, axis=0, keepdims=True) * edge_scale
        vec[2:3, :] += jnp.sum(grad, axis=0, keepdims=True) * edge_scale
        edge_out[at, :] = (cot + mm_nt(grad_pre, first[...])).astype(BF16)
        sums[...] += mm(hot_t[:, at], grad_pre)
        ges_ref[...] += mm_tn(active_s[at, :], grad_out) * edge_scale
        gef_ref[pl.ds(0, latent), :] += mm_tn(el_ref[at, :], grad_pre) * edge_scale

    received = sums[pl.ds(0, nodes), :].astype(BF16)
    sent = sums[pl.ds(nodes, nodes + halo), :].astype(BF16)
    gef_ref[pl.ds(latent, latent), :] = mm_tn(table[...], sent) * edge_scale
    gef_ref[pl.ds(2 * latent, latent), :] = mm_tn(nl, received) * edge_scale
    back = mm_nt(sent, sender[...])
    node_part[...] += back[:nodes] + mm_nt(received, receiver[...])
    slots = halo // peers
    pieces = jnp.concatenate(
        [
            back[nodes:].reshape(peers, slots, latent),
            jnp.broadcast_to(vec[...][None], (peers, 8, latent)),
        ],
        axis=1,
    )
    ret_ref[...] = pieces.astype(BF16)


def reduce_kernel(regions, subs, k, count, *refs):
    grads = refs[:count]
    ret_ref, part_ref, slots_ref = refs[count : count + 3]
    refs = refs[count + 3 :]
    node_out, vec_out = refs[:2]
    outs = refs[2 : 2 + count]
    refs = refs[2 + count :]
    got = refs[0]
    bufs = [refs[1 + 6 * c : 7 + 6 * c] for c in range(count)]
    ret_send, ret_recv, near_send, near_recv, far_send, far_recv = refs[1 + 6 * count :]

    peers = regions * subs
    outer = regions // 2
    region = lax.axis_index("region")
    sub = lax.axis_index("sub")
    me = region * subs + sub
    inner = lax.rem(region, 2)
    place_o = region // 2
    barrier = greet_all(me, peers, subs)

    def own(c, q, s):
        m = outs[c].shape[0]
        row = pl.multiple_of((q * subs + s) * m, 8)
        return fold(grads[c][pl.ds(row, m), :], k)

    for c in range(count):
        a1 = bufs[c][0]

        @pl.loop(0, regions)
        def _(q, c=c, a1=a1):
            a1[q] = own(c, q, 1 - sub).astype(BF16)

    pl.semaphore_wait(barrier, peers - 1)

    def near(c, stage, src, dst, target):
        return pltpu.make_async_remote_copy(
            src_ref=src,
            dst_ref=dst,
            send_sem=near_send.at[c, stage],
            recv_sem=near_recv.at[c, stage],
            device_id=target,
            device_id_type=MESH,
        )

    def stage_1(c):
        return near(c, 0, bufs[c][0], bufs[c][1], {"region": region, "sub": 1 - sub})

    def stage_2(c):
        other = region + 1 - 2 * inner
        return near(c, 1, bufs[c][2], bufs[c][3], {"region": other, "sub": sub})

    def stage_3(c, d, target, slot):
        return pltpu.make_async_remote_copy(
            src_ref=bufs[c][4].at[target],
            dst_ref=bufs[c][5].at[slot],
            send_sem=far_send.at[c, d],
            recv_sem=far_recv.at[c, d],
            device_id={"region": target * 2 + inner, "sub": sub},
            device_id_type=MESH,
        )

    def back(d, target, slot):
        return pltpu.make_async_remote_copy(
            src_ref=ret_ref.at[target],
            dst_ref=got.at[slot],
            send_sem=ret_send.at[d],
            recv_sem=ret_recv.at[d],
            device_id=place(target, subs),
            device_id_type=MESH,
        )

    for c in range(count):
        stage_1(c).start()

    @pl.loop(1, peers)
    def _(d):
        back(d, lax.rem(me + d, peers), me).start()

    got[me] = ret_ref[me]

    for c in range(count):
        b1, a2 = bufs[c][1:3]
        stage_1(c).wait_recv()

        @pl.loop(0, outer)
        def _(o, c=c, b1=b1, a2=a2):
            q = o * 2 + 1 - inner
            a2[o] = (own(c, q, sub) + b1[q].astype(F32)).astype(BF16)

        stage_2(c).start()

    for c in range(count):
        b1, b2, a3 = bufs[c][1], bufs[c][3], bufs[c][4]
        stage_2(c).wait_recv()

        @pl.loop(0, outer)
        def _(o, c=c, b1=b1, b2=b2, a3=a3):
            q = o * 2 + inner
            a3[o] = (own(c, q, sub) + b1[q].astype(F32) + b2[o].astype(F32)).astype(BF16)

        @pl.loop(1, outer)
        def _(d, c=c):
            stage_3(c, d, lax.rem(place_o + d, outer), place_o).start()

    @pl.loop(1, peers)
    def _(d):
        back(d, lax.rem(me + d, peers), lax.rem(me + peers - d, peers)).wait_recv()

    nodes, latent = part_ref.shape
    arrived = got[...].astype(F32)
    vec_out[...] = jnp.sum(arrived[:, 8:], axis=0)
    returned = arrived[:, :8].reshape(peers * 8, latent).astype(BF16)
    spread = one_hot(
        lax.broadcasted_iota(jnp.int32, (nodes, peers * 8), 0) == slots_ref[...]
    )
    node_out[...] = (part_ref[...] + mm(spread, returned)).astype(BF16)

    for c in range(count):
        b1, b2, b3 = bufs[c][1], bufs[c][3], bufs[c][5]

        @pl.loop(1, outer)
        def _(d, c=c):
            stage_3(
                c, d, lax.rem(place_o + d, outer), lax.rem(place_o + outer - d, outer)
            ).wait_recv()

        result = own(c, region, sub) + b1[region].astype(F32) + b2[place_o].astype(F32)

        def add(d, value, b3=b3):
            return value + b3[lax.rem(place_o + d, outer)].astype(F32)

        outs[c][...] = unfold(lax.fori_loop(1, outer, add, result), k)

    for c in range(count):
        stage_1(c).wait_send()
        stage_2(c).wait_send()

        @pl.loop(1, outer)
        def _(d, c=c):
            stage_3(c, d, lax.rem(place_o + d, outer), place_o).wait_send()

    @pl.loop(1, peers)
    def _(d):
        back(d, lax.rem(me + d, peers), me).wait_send()


def in_vmem(count):
    return [pl.BlockSpec(memory_space=pltpu.VMEM)] * count


def on_device(
    regions,
    subs,
    node_latent,
    edge_latent,
    node_cot,
    edge_cot,
    send_rows,
    edge_sender,
    edge_receiver,
    edge_first,
    edge_second,
    edge_bias,
    edge_gain,
    edge_shift,
    node_first,
    node_second,
    node_bias,
    node_gain,
):
    peers = regions * subs
    nodes, latent = node_latent.shape
    edges = edge_latent.shape[0]
    slots = send_rows.shape[2]
    halo_rows = peers * slots
    total = 2 * nodes + halo_rows
    shape = jax.ShapeDtypeStruct

    halo = pl.pallas_call(
        functools.partial(halo_kernel, regions, subs),
        out_shape=shape((halo_rows, latent), BF16),
        in_specs=in_vmem(2),
        out_specs=pl.BlockSpec(memory_space=pltpu.VMEM),
        scratch_shapes=[
            pltpu.VMEM((peers, 2 * slots, latent // 2), BF16),
            pltpu.VMEM((peers, 2 * slots, latent // 2), BF16),
            pltpu.SemaphoreType.DMA((peers,)),
            pltpu.SemaphoreType.DMA((peers,)),
        ],
        compiler_params=pltpu.CompilerParams(collective_id=0, has_side_effects=True),
    )(send_rows.reshape(halo_rows, 1), node_latent)

    tile = math.gcd(edges, 512)
    ends = (edge_receiver, edge_sender + nodes)
    row = lambda x: x.reshape(1, latent)
    edge_grad, part, ret, gef, ges, gnf, gns = pl.pallas_call(
        functools.partial(compute_kernel, peers, tile),
        out_shape=(
            shape((edges, latent), BF16),
            shape((nodes, latent), F32),
            shape((peers, slots + 8, latent), BF16),
            shape(edge_first.shape, F32),
            shape(edge_second.shape, F32),
            shape(node_first.shape, F32),
            shape(node_second.shape, F32),
        ),
        in_specs=in_vmem(16),
        out_specs=tuple(in_vmem(7)),
        scratch_shapes=[
            pltpu.VMEM((edges, total), BF16),
            pltpu.VMEM((total, edges), BF16),
            pltpu.VMEM((nodes + halo_rows, latent), BF16),
            pltpu.VMEM((total, latent), BF16),
            pltpu.VMEM((edges, latent), BF16),
            pltpu.VMEM((edges, latent), F32),
            pltpu.VMEM((edges, latent), F32),
            pltpu.VMEM((edges, 1), F32),
            pltpu.VMEM((nodes, latent), F32),
            pltpu.VMEM((total, latent), F32),
            pltpu.VMEM((8, latent), F32),
        ],
        compiler_params=pltpu.CompilerParams(vmem_limit_bytes=VMEM_LIMIT),
    )(
        node_latent,
        edge_latent,
        node_cot,
        edge_cot,
        halo,
        jnp.stack(ends, axis=1),
        jnp.stack(ends, axis=0),
        edge_first,
        edge_second,
        row(edge_bias),
        row(edge_gain),
        row(edge_shift),
        node_first,
        node_second,
        row(node_bias),
        row(node_gain),
    )

    partials = (gns, gnf, ges, gef)
    shares = [g.shape[0] // peers for g in partials]
    k = 1 if all(m % 16 == 0 for m in shares) else 2
    outer = regions // 2
    scratch = [pltpu.VMEM((peers, slots + 8, latent), BF16)]
    for m in shares:
        block = (m * k, latent // k)
        for lead in (regions, regions, outer, outer, outer, outer):
            scratch.append(pltpu.VMEM((lead,) + block, BF16))
    count = len(partials)
    sem = pltpu.SemaphoreType.DMA
    scratch += [sem((peers,)), sem((peers,)), sem((count, 2)), sem((count, 2))]
    scratch += [sem((count, outer)), sem((count, outer))]
    node_grad, vectors, gns, gnf, ges, gef = pl.pallas_call(
        functools.partial(reduce_kernel, regions, subs, k, count),
        out_shape=(
            shape((nodes, latent), BF16),
            shape((8, latent), F32),
            *(shape((m, latent), F32) for m in shares),
        ),
        in_specs=in_vmem(count + 3),
        out_specs=tuple(in_vmem(count + 2)),
        scratch_shapes=scratch,
        compiler_params=pltpu.CompilerParams(
            collective_id=1, has_side_effects=True, vmem_limit_bytes=VMEM_LIMIT
        ),
    )(*partials, ret, part, send_rows.reshape(1, halo_rows))

    width = latent // peers
    start = (lax.axis_index("region") * subs + lax.axis_index("sub")) * width
    mine = lax.dynamic_slice(vectors, (0, start), (8, width))
    return node_grad, edge_grad, gef, ges, mine[0:3], gnf, gns, mine[3:5]


def solution(mesh):
    spread = P(("group", "region", "sub"), None)
    flat = P(("group", "region", "sub"))
    vector = P("group", ("region", "sub"))
    return jax.shard_map(
        functools.partial(on_device, mesh.shape["region"], mesh.shape["sub"]),
        mesh=mesh,
        in_specs=(
            spread,
            spread,
            spread,
            spread,
            P(("group", "region", "sub"), None, None),
            flat,
            flat,
        )
        + (P(),) * 9,
        out_specs=(spread, spread, spread, spread, vector, spread, spread, vector),
        check_vma=False,
    )
```

time: 466 us -> 91.5 us (0.20)
  waiting for transfers between devices: 288 us -> 0 us
  Pallas kernels: 0 us -> 74.7 us
  other arithmetic: 58.2 us -> 1.33 us
  local copies, waits for them, and re-layouts: 55.3 us -> 14.3 us
  matrix products: 35.2 us -> 0 us
  between operations: 14.6 us -> 0.68 us
  starting transfers between devices: 13.9 us -> 0 us
    reduce_scatter x4 -> x0, waiting for transfers between devices: 252 us -> none  [the longest x1 70 us: on_device(): lax.psum_scatter(partials[0], ('region', 'sub'), scatter_dimension=0, til...]
    pallas_call x0 -> x3, Pallas kernels: none -> 74.7 us  [the longest x1 42.2 us: on_device(): pl.pallas_call(functools.partial(reduce_kernel, regions, subs, k, count),...]
    unnamed x8 -> x0, waiting for transfers between devices: 36.2 us -> none
    scatter-add x4 -> x0, other arithmetic: 36 us -> none  [the longest x1 12.2 us: on_device(): jax.ops.segment_sum(e_input_grad[:, 2 * latent:], edge_receiver, num_segm...]
    dot_general x12 -> x0, matrix products: 35.2 us -> none  [the longest x2 9.95 us: mlp_backward(): grad_first = jnp.dot(inputs.T, grad_pre, preferred_element_type=jnp.float32)]
    gather x5 -> x0, local copies, waits for them, and re-layouts: 22 us -> none  [the longest x2 8.68 us: on_device(): n_input_grad[:, latent:][edge_receiver]]
    unnamed x94 -> x6, local copies, waits for them, and re-layouts: 25.5 us -> 8.5 us
    all_to_all x2 -> x0, starting transfers between devices: 13.5 us -> none  [the longest x1 7.39 us: on_device(): lax.all_to_all(outgoing, ('region', 'sub'), split_axis=0, concat_axis=0,...]
  transfers between devices with their start and end apart: 8 -> 0, of which waited for: 5 -> 0; matrix products, arithmetic and copies ran while one was open for 18% -> 0% of each run, Pallas kernels for 0% -> 0%
where the time goes in v1:
time: 91.5 us; the launch traced here: 91 us
  Pallas kernels  74.7 us (82%)
  local copies, waits for them, and re-layouts  14.3 us (16%)
  other arithmetic  1.33 us (1%)
    pallas_call x1, Pallas kernels, on_device(): pl.pallas_call(functools.partial(reduce_kernel, regions, subs, k, count),...  42.2 us
    pallas_call x1, Pallas kernels, on_device(): pl.pallas_call(functools.partial(compute_kernel, peers, tile), out_shape=...  21.5 us
    pallas_call x1, Pallas kernels, on_device(): pl.pallas_call(functools.partial(halo_kernel, regions, subs), out_shape=s...  11 us
    unnamed x6, local copies, waits for them, and re-layouts  8.5 us
    another operation x3, local copies, waits for them, and re-layouts, on_device(): jnp.stack(ends, axis=1)  1.89 us

profile of v1, /device:TPU:0, one launch (start us, length us, event | category | flops | bytes accessed | tf_op | source)
XLA Modules:
  0.0 91.0 jit_solution(13044210229003007940)
XLA Ops:
  0.6 0.7 stack.21
  1.3 0.7 stack.18
  2.0 0.8 copy.32
  2.8 0.6 reshape.43.refs_6_
  3.4 0.7 broadcast_add_fusion
  4.1 0.6 pad_add_fusion.1.rows_ref
  4.8 0.7 reshape.44.rows_ref
  5.5 11.0 %shard_map.215.halo_ref = bf16[128,512]{1,0:T(8,128)(2,1)} custom-call(s32[128,1]{1,0:T(8,128)} %reshape.44.rows_ref, bf16[192,512]{1,0:T(8,128)(2,1)} %nl_ref.1), custom_call_target="tpu_custom_call" | custom-call | tf_op jit(solution)/shard_map/pallas_call | solution.py:434
  16.4 1.2 %copy.34.cols_ref = s32[1536,2]{1,0:T(8,128)} copy(s32[1536,2]{0,1:T(2,128)S(1)} %pad_add_fusion) | data formatting | bytes 24576 | tf_op jit(solution)/shard_map/stack | solution.py:484
  17.6 21.5 %shard_map.216 = (bf16[1536,512]{1,0:T(8,128)(2,1)}, f32[192,512]{1,0:T(8,128)}, bf16[16,16,512]{2,1,0:T(8,128)(2,1)}, f32[1536,512]{1,0:T(8,128)}, f32[512,512]...) custom-call(bf16[192,512]{1,0:T(8,128)(2,1)} %nl_ref.1, bf16[1536,512]{1,0:T(8,128)(2,1)} %el_ref.1, ...), custom_call_target="tpu_custom_call" | custom-call | tf_op jit(solution)/shard_map/pallas_call | solution.py:451
  39.1 42.2 %shard_map.217 = (bf16[192,512]{1,0:T(8,128)(2,1)}, f32[8,512]{1,0:T(8,128)}, f32[32,512]{1,0:T(8,128)}, f32[64,512]{1,0:T(8,128)}, f32[32,512]{1,0:T(8,128)}, /*index=5*/f32[96,512]{1,0:T(8,128)}) custom-call(f32[512,512]{1,0:T(8,128)} %get-tuple-element.21.refs_0_, f32[1024,512]{1,0:T(8,128)} %get-tuple-element.22.refs_1_, ...), custom_call_target="tpu_custom_call" | custom-call | tf_op jit(solution)/shard_map/pallas_call | solution.py:510
  81.3 0.8 constant_dynamic-slice_fusion
  82.1 0.6 slice.7
  82.7 0.6 slice.6
  83.2 1.6 %copy.41 = bf16[192,512]{1,0:T(8,128)(2,1)} copy(bf16[192,512]{1,0:T(8,128)(2,1)} %get-tuple-element.42) | data formatting | bytes 393216
  84.9 1.6 %copy.42 = f32[96,512]{1,0:T(8,128)} copy(f32[96,512]{1,0:T(8,128)} %get-tuple-element.44) | data formatting | bytes 393216
  86.5 1.5 %copy.43 = f32[32,512]{1,0:T(8,128)} copy(f32[32,512]{1,0:T(8,128)} %get-tuple-element.45) | data formatting | bytes 131072
  87.9 1.6 %copy.44 = f32[64,512]{1,0:T(8,128)} copy(f32[64,512]{1,0:T(8,128)} %get-tuple-element.47) | data formatting | bytes 262144
  89.5 1.5 %copy.45 = f32[32,512]{1,0:T(8,128)} copy(f32[32,512]{1,0:T(8,128)} %get-tuple-element.48) | data formatting | bytes 131072
  (3 shorter events, 0.0 us)

commit v2 on v1

v2 whole, which is shorter than its diff:
```python
import functools
import math

import jax
import jax.numpy as jnp
from jax import lax
from jax.experimental import pallas as pl
from jax.experimental.pallas import tpu as pltpu
from jax.sharding import PartitionSpec as P

MESH = pl.DeviceIdType.MESH
F32 = jnp.float32
BF16 = jnp.bfloat16
VMEM_LIMIT = 56 * 1024 * 1024


def mm(a, b):
    return jnp.dot(a, b, preferred_element_type=F32)


def mm_nt(a, b):
    return lax.dot_general(a, b, (((1,), (1,)), ((), ())), preferred_element_type=F32)


def mm_tn(a, b):
    return lax.dot_general(a, b, (((0,), (0,)), ((), ())), preferred_element_type=F32)


def one_hot(mask):
    return jnp.where(mask, 1.0, 0.0).astype(BF16)


def fold(x, k):
    if k == 1:
        return x
    w = x.shape[-1] // k
    return jnp.concatenate([x[..., j * w : (j + 1) * w] for j in range(k)], axis=-2)


def unfold(x, k):
    if k == 1:
        return x
    m = x.shape[-2] // k
    return jnp.concatenate([x[..., j * m : (j + 1) * m, :] for j in range(k)], axis=-1)


def place(index, subs):
    return {"region": index // subs, "sub": lax.rem(index, subs)}


def greet_all(me, peers, subs):
    barrier = pltpu.get_barrier_semaphore()

    @pl.loop(1, peers)
    def _(d):
        pl.semaphore_signal(
            barrier, inc=1, device_id=place(lax.rem(me + d, peers), subs), device_id_type=MESH
        )

    return barrier


def layer_norm(out):
    centred = out - jnp.mean(out, axis=-1, keepdims=True)
    inverse = lax.rsqrt(jnp.mean(centred * centred, axis=-1, keepdims=True) + 1e-05)
    return centred * inverse, inverse


def norm_backward(upstream, gain, normed, inverse):
    grad_norm = upstream * gain
    centred = grad_norm - jnp.mean(grad_norm, axis=-1, keepdims=True)
    share = jnp.mean(grad_norm * normed, axis=-1, keepdims=True)
    return (inverse * (centred - normed * share)).astype(BF16)


def activate(before):
    s = jax.nn.sigmoid(before)
    return (before * s).astype(BF16), s + before * s * (1.0 - s)


def layer_kernel(
    regions,
    subs,
    tile,
    k,
    chunks,
    nl_ref,
    el_ref,
    nc_ref,
    ec_ref,
    slots_ref,
    es_idx,
    er_idx,
    ef_ref,
    es_ref,
    eb_ref,
    eg_ref,
    esh_ref,
    nf_ref,
    ns_ref,
    nb_ref,
    ng_ref,
    edge_out,
    small_out,
    hot,
    hot_t,
    cols,
    table,
    projected,
    active_s,
    dsilu_s,
    normed_s,
    inverse_s,
    agg,
    sums,
    vec,
    node_part,
    gns_ref,
    gnf_ref,
    ges_ref,
    gef_ref,
    halo_sent,
    halo_got,
    ret_ref,
    got,
    halo_send,
    halo_recv,
    ret_send,
    ret_recv,
    near_send,
    near_recv,
    far_send,
    far_recv,
    *bufs,
):
    peers = regions * subs
    outer = regions // 2
    region = lax.axis_index("region")
    sub = lax.axis_index("sub")
    me = region * subs + sub
    inner = lax.rem(region, 2)
    place_o = region // 2

    edges, latent = el_ref.shape
    nodes = nl_ref.shape[0]
    halo = slots_ref.shape[1]
    slots = halo // peers
    total = 2 * nodes + halo
    edge_scale = 1.0 / math.sqrt(edges * peers)
    node_scale = 1.0 / math.sqrt(nodes * peers)
    steps = edges // tile
    first = ef_ref.at[pl.ds(0, latent)]
    sender = ef_ref.at[pl.ds(latent, latent)]
    receiver = ef_ref.at[pl.ds(2 * latent, latent)]
    grads = (gns_ref, gnf_ref, ges_ref, gef_ref)
    shares = [g.shape[0] // peers for g in grads]
    starts = [sum(shares[:j]) for j in range(5)]

    barrier = greet_all(me, peers, subs)
    nl = nl_ref[...]
    slot_col = jnp.transpose(jnp.broadcast_to(slots_ref[...].astype(F32), (8, halo)))[:, 0:1]
    node_iota = lax.broadcasted_iota(jnp.int32, (halo, nodes), 1).astype(F32)
    picked = mm(one_hot(node_iota == slot_col), nl)
    halo_sent[...] = fold(picked.reshape(peers, slots, latent), 2).astype(BF16)
    pl.semaphore_wait(barrier, peers - 1)

    def halo_copy(d, target, slot):
        return pltpu.make_async_remote_copy(
            src_ref=halo_sent.at[target],
            dst_ref=halo_got.at[slot],
            send_sem=halo_send.at[d],
            recv_sem=halo_recv.at[d],
            device_id=place(target, subs),
            device_id_type=MESH,
        )

    @pl.loop(1, peers)
    def _(d):
        halo_copy(d, lax.rem(me + d, peers), me).start()

    halo_got[me] = halo_sent[me]
    table[pl.ds(0, nodes), :] = nl
    projected[pl.ds(0, nodes), :] = mm(nl, receiver[...]).astype(BF16)
    agg[...] = jnp.zeros_like(agg)
    sums[...] = jnp.zeros_like(sums)
    vec[...] = jnp.zeros_like(vec)
    cols[...] = jnp.transpose(
        jnp.concatenate(
            [
                jnp.broadcast_to(er_idx[...], (4, edges)),
                jnp.broadcast_to(es_idx[...] + nodes, (4, edges)),
            ],
            axis=0,
        ).astype(F32)
    )

    @pl.loop(0, steps)
    def _(t):
        at = pl.ds(pl.multiple_of(t * tile, tile), tile)
        iota = lax.broadcasted_iota(jnp.int32, (tile, total), 1).astype(F32)
        hot[at, :] = one_hot((cols[at, 0:1] == iota) | (cols[at, 4:5] == iota))
        iota_t = lax.broadcasted_iota(jnp.int32, (total, tile), 0)
        hot_t[:, at] = one_hot((er_idx[:, at] == iota_t) | (es_idx[:, at] + nodes == iota_t))
        dsilu_s[at, :] = mm(el_ref[at, :], first[...]) + eb_ref[...]

    @pl.loop(1, peers)
    def _(d):
        halo_copy(d, lax.rem(me + d, peers), lax.rem(me + peers - d, peers)).wait_recv()

    table[pl.ds(nodes, halo), :] = (
        unfold(halo_got[...].astype(F32), 2).reshape(halo, latent).astype(BF16)
    )
    projected[pl.ds(nodes, nodes + halo), :] = mm(table[...], sender[...]).astype(BF16)

    @pl.loop(0, steps)
    def _(t):
        at = pl.ds(pl.multiple_of(t * tile, tile), tile)
        active, dsilu = activate(dsilu_s[at, :] + mm(hot[at, :], projected[...]))
        active_s[at, :] = active
        dsilu_s[at, :] = dsilu
        normed, inverse = layer_norm(mm(active, es_ref[...]))
        normed_s[at, :] = normed
        inverse_s[at, :] = inverse
        message = (normed * eg_ref[...] + esh_ref[...]).astype(BF16)
        agg[...] += mm(hot_t[pl.ds(0, nodes), at], message)

    def own(c, q, s):
        g, col, width = chunks[c]
        m = shares[g]
        row = pl.multiple_of((q * subs + s) * m, 8)
        return fold(grads[g][pl.ds(row, m), pl.ds(col, width)], k)

    def near(c, stage, src, dst, target):
        return pltpu.make_async_remote_copy(
            src_ref=src,
            dst_ref=dst,
            send_sem=near_send.at[c, stage],
            recv_sem=near_recv.at[c, stage],
            device_id=target,
            device_id_type=MESH,
        )

    def of(c):
        return bufs[6 * c : 6 * c + 6]

    def copy_1(c):
        return near(c, 0, of(c)[0], of(c)[1], {"region": region, "sub": 1 - sub})

    def copy_2(c):
        other = region + 1 - 2 * inner
        return near(c, 1, of(c)[2], of(c)[3], {"region": other, "sub": sub})

    def copy_3(c, d, target, slot):
        return pltpu.make_async_remote_copy(
            src_ref=of(c)[4].at[target],
            dst_ref=of(c)[5].at[slot],
            send_sem=far_send.at[c, d],
            recv_sem=far_recv.at[c, d],
            device_id={"region": target * 2 + inner, "sub": sub},
            device_id_type=MESH,
        )

    def ret_copy(d, target, slot):
        return pltpu.make_async_remote_copy(
            src_ref=ret_ref.at[target],
            dst_ref=got.at[slot],
            send_sem=ret_send.at[d],
            recv_sem=ret_recv.at[d],
            device_id=place(target, subs),
            device_id_type=MESH,
        )

    def stage_1(c):
        a1 = of(c)[0]

        @pl.loop(0, regions)
        def _(q):
            a1[q] = own(c, q, 1 - sub).astype(BF16)

        copy_1(c).start()

    def stage_2(c):
        b1, a2 = of(c)[1:3]
        copy_1(c).wait_recv()

        @pl.loop(0, outer)
        def _(o):
            q = o * 2 + 1 - inner
            a2[o] = (own(c, q, sub) + b1[q].astype(F32)).astype(BF16)

        copy_2(c).start()

    def stage_3(c):
        b1, b2, a3 = of(c)[1], of(c)[3], of(c)[4]
        copy_2(c).wait_recv()

        @pl.loop(0, outer)
        def _(o):
            q = o * 2 + inner
            a3[o] = (own(c, q, sub) + b1[q].astype(F32) + b2[o].astype(F32)).astype(BF16)

        @pl.loop(1, outer)
        def _(d):
            copy_3(c, d, lax.rem(place_o + d, outer), place_o).start()

    def finish(c):
        b1, b2, b3 = of(c)[1], of(c)[3], of(c)[5]

        @pl.loop(1, outer)
        def _(d):
            source = lax.rem(place_o + outer - d, outer)
            copy_3(c, d, lax.rem(place_o + d, outer), source).wait_recv()

        result = own(c, region, sub) + b1[region].astype(F32) + b2[place_o].astype(F32)

        def add(d, value):
            return value + b3[lax.rem(place_o + d, outer)].astype(F32)

        g, col, width = chunks[c]
        value = unfold(lax.fori_loop(1, outer, add, result), k)
        small_out[pl.ds(starts[g], shares[g]), pl.ds(col, width)] = value

    node_chunks = [c for c, (g, _, _) in enumerate(chunks) if g < 2]
    second_chunks = [c for c, (g, _, _) in enumerate(chunks) if g == 2]
    first_chunks = [c for c, (g, _, _) in enumerate(chunks) if g == 3]

    aggregate = agg[...].astype(BF16)
    top = nf_ref.at[pl.ds(0, latent)]
    low = nf_ref.at[pl.ds(latent, latent)]
    before = mm(nl, top[...]) + mm(aggregate, low[...]) + nb_ref[...]
    active, dsilu = activate(before)
    normed, inverse = layer_norm(mm(active, ns_ref[...]))
    cot = nc_ref[...].astype(F32)
    grad_out = norm_backward(cot, ng_ref[...], normed, inverse)
    grad_before = mm_nt(grad_out, ns_ref[...]) * dsilu
    grad_pre = grad_before.astype(BF16)
    gns_ref[...] = mm_tn(active, grad_out) * node_scale
    gnf_ref[pl.ds(0, latent), :] = mm_tn(nl, grad_pre) * node_scale
    gnf_ref[pl.ds(latent, latent), :] = mm_tn(aggregate, grad_pre) * node_scale
    for c in node_chunks:
        stage_1(c)
    node_part[...] = cot + mm_nt(grad_pre, top[...])
    projected[pl.ds(0, nodes), :] = mm_nt(grad_pre, low[...]).astype(BF16)
    vec[3:4, :] = jnp.sum(grad_before, axis=0, keepdims=True) * node_scale
    vec[4:5, :] = jnp.sum(cot * normed, axis=0, keepdims=True) * node_scale
    gef_ref[pl.ds(0, latent), :] = jnp.zeros((latent, latent), F32)
    ges_ref[...] = jnp.zeros_like(ges_ref)

    @pl.loop(0, steps)
    def _(t):
        at = pl.ds(pl.multiple_of(t * tile, tile), tile)
        cot = ec_ref[at, :].astype(F32)
        grad = cot + mm(hot[at, pl.ds(0, nodes)], projected[pl.ds(0, nodes), :])
        normed = normed_s[at, :]
        grad_out = norm_backward(grad, eg_ref[...], normed, inverse_s[at, :])
        grad_before = mm_nt(grad_out, es_ref[...]) * dsilu_s[at, :]
        grad_pre = grad_before.astype(BF16)
        vec[0:1, :] += jnp.sum(grad_before, axis=0, keepdims=True) * edge_scale
        vec[1:2, :] += jnp.sum(grad * normed, axis=0, keepdims=True) * edge_scale
        vec[2:3, :] += jnp.sum(grad, axis=0, keepdims=True) * edge_scale
        edge_out[at, :] = (cot + mm_nt(grad_pre, first[...])).astype(BF16)
        sums[...] += mm(hot_t[:, at], grad_pre)
        ges_ref[...] += mm_tn(active_s[at, :], grad_out) * edge_scale
        gef_ref[pl.ds(0, latent), :] += mm_tn(el_ref[at, :], grad_pre) * edge_scale

        @pl.when(t == 0)
        def _():
            for c in node_chunks:
                stage_2(c)

        @pl.when(t == min(1, steps - 1))
        def _():
            for c in node_chunks:
                stage_3(c)

    for c in second_chunks:
        stage_1(c)
    received = sums[pl.ds(0, nodes), :].astype(BF16)
    sent = sums[pl.ds(nodes, nodes + halo), :].astype(BF16)
    gef_ref[pl.ds(latent, latent), :] = mm_tn(table[...], sent) * edge_scale
    gef_ref[pl.ds(2 * latent, latent), :] = mm_tn(nl, received) * edge_scale
    for c in first_chunks:
        stage_1(c)
    back = mm_nt(sent, sender[...])
    ret_ref[...] = jnp.concatenate(
        [
            back[nodes:].reshape(peers, slots, latent),
            jnp.broadcast_to(vec[...][None], (peers, 8, latent)),
        ],
        axis=1,
    ).astype(BF16)

    @pl.loop(1, peers)
    def _(d):
        ret_copy(d, lax.rem(me + d, peers), me).start()

    got[me] = ret_ref[me]
    for c in second_chunks + first_chunks:
        stage_2(c)
    node_part[...] += back[:nodes] + mm_nt(received, receiver[...])
    for c in node_chunks:
        finish(c)
    for c in second_chunks + first_chunks:
        stage_3(c)

    @pl.loop(1, peers)
    def _(d):
        ret_copy(d, lax.rem(me + d, peers), lax.rem(me + peers - d, peers)).wait_recv()

    arrived = got[...].astype(F32)
    vectors = jnp.sum(arrived[:, slots:], axis=0)
    width = latent // peers
    mine = jnp.zeros((8, width), F32)
    for p in range(peers):
        mine = jnp.where(me == p, vectors[:, p * width : (p + 1) * width], mine)
    small_out[pl.ds(starts[4], 8), pl.ds(0, width)] = mine
    returned = arrived[:, :slots].reshape(halo, latent).astype(BF16)
    spread = one_hot(lax.broadcasted_iota(jnp.int32, (nodes, halo), 0) == slots_ref[...])
    small_out[pl.ds(starts[4] + 8, nodes), :] = node_part[...] + mm(spread, returned)
    for c in second_chunks + first_chunks:
        finish(c)

    for c in range(len(chunks)):
        copy_1(c).wait_send()
        copy_2(c).wait_send()

        @pl.loop(1, outer)
        def _(d, c=c):
            copy_3(c, d, lax.rem(place_o + d, outer), place_o).wait_send()

    @pl.loop(1, peers)
    def _(d):
        halo_copy(d, lax.rem(me + d, peers), me).wait_send()
        ret_copy(d, lax.rem(me + d, peers), me).wait_send()


def split_kernel(small_ref, node_out, gns_out, gnf_out, ges_out, gef_out, ev_out, nv_out):
    row = 0
    for out in (gns_out, gnf_out, ges_out, gef_out):
        out[...] = small_ref[pl.ds(row, out.shape[0]), :]
        row += out.shape[0]
    width = ev_out.shape[1]
    vectors = small_ref[pl.ds(row, 8), :]
    ev_out[...] = vectors[0:3, :width]
    nv_out[...] = vectors[3:5, :width]
    node_out[...] = small_ref[pl.ds(row + 8, node_out.shape[0]), :].astype(BF16)


def in_vmem(count):
    return [pl.BlockSpec(memory_space=pltpu.VMEM)] * count


def on_device(
    regions,
    subs,
    node_latent,
    edge_latent,
    node_cot,
    edge_cot,
    send_rows,
    edge_sender,
    edge_receiver,
    edge_first,
    edge_second,
    edge_bias,
    edge_gain,
    edge_shift,
    node_first,
    node_second,
    node_bias,
    node_gain,
):
    peers = regions * subs
    nodes, latent = node_latent.shape
    edges = edge_latent.shape[0]
    slots = send_rows.shape[2]
    halo = peers * slots
    total = 2 * nodes + halo
    shape = jax.ShapeDtypeStruct
    tile = math.gcd(edges, 512)
    row = lambda x: x.reshape(1, -1)

    weights = (node_second, node_first, edge_second, edge_first)
    shares = [w.shape[0] // peers for w in weights]
    k = 1 if all(m % 16 == 0 for m in shares) else 2
    half = latent // 2
    chunks = ((0, 0, latent), (1, 0, half), (1, half, half))
    chunks += ((2, 0, latent), (3, 0, half), (3, half, half))
    outer = regions // 2
    sem = pltpu.SemaphoreType.DMA
    count = len(chunks)
    scratch = [
        pltpu.VMEM((edges, total), BF16),
        pltpu.VMEM((total, edges), BF16),
        pltpu.VMEM((edges, 8), F32),
        pltpu.VMEM((nodes + halo, latent), BF16),
        pltpu.VMEM((total, latent), BF16),
        pltpu.VMEM((edges, latent), BF16),
        pltpu.VMEM((edges, latent), F32),
        pltpu.VMEM((edges, latent), F32),
        pltpu.VMEM((edges, 1), F32),
        pltpu.VMEM((nodes, latent), F32),
        pltpu.VMEM((total, latent), F32),
        pltpu.VMEM((8, latent), F32),
        pltpu.VMEM((nodes, latent), F32),
        *(pltpu.VMEM(w.shape, F32) for w in weights),
        pltpu.VMEM((peers, 2 * slots, half), BF16),
        pltpu.VMEM((peers, 2 * slots, half), BF16),
        pltpu.VMEM((peers, slots + 8, latent), BF16),
        pltpu.VMEM((peers, slots + 8, latent), BF16),
        sem((peers,)),
        sem((peers,)),
        sem((peers,)),
        sem((peers,)),
        sem((count, 2)),
        sem((count, 2)),
        sem((count, outer)),
        sem((count, outer)),
    ]
    for g, _, width in chunks:
        for lead in (regions, regions, outer, outer, outer, outer):
            scratch.append(pltpu.VMEM((lead, shares[g] * k, width // k), BF16))
    small_rows = sum(shares) + 8 + nodes
    edge_grad, small = pl.pallas_call(
        functools.partial(layer_kernel, regions, subs, tile, k, chunks),
        out_shape=(shape((edges, latent), BF16), shape((small_rows, latent), F32)),
        in_specs=in_vmem(16),
        out_specs=tuple(in_vmem(2)),
        scratch_shapes=scratch,
        compiler_params=pltpu.CompilerParams(
            collective_id=0, has_side_effects=True, vmem_limit_bytes=VMEM_LIMIT
        ),
    )(
        node_latent,
        edge_latent,
        node_cot,
        edge_cot,
        row(send_rows),
        row(edge_sender),
        row(edge_receiver),
        edge_first,
        edge_second,
        row(edge_bias),
        row(edge_gain),
        row(edge_shift),
        node_first,
        node_second,
        row(node_bias),
        row(node_gain),
    )
    width = latent // peers
    node_grad, gns, gnf, ges, gef, ev, nv = pl.pallas_call(
        split_kernel,
        out_shape=(
            shape((nodes, latent), BF16),
            *(shape((m, latent), F32) for m in shares),
            shape((3, width), F32),
            shape((2, width), F32),
        ),
        in_specs=in_vmem(1),
        out_specs=tuple(in_vmem(7)),
    )(small)
    return node_grad, edge_grad, gef, ges, ev, gnf, gns, nv


def solution(mesh):
    spread = P(("group", "region", "sub"), None)
    flat = P(("group", "region", "sub"))
    vector = P("group", ("region", "sub"))
    return jax.shard_map(
        functools.partial(on_device, mesh.shape["region"], mesh.shape["sub"]),
        mesh=mesh,
        in_specs=(
            spread,
            spread,
            spread,
            spread,
            P(("group", "region", "sub"), None, None),
            flat,
            flat,
        )
        + (P(),) * 9,
        out_specs=(spread, spread, spread, spread, vector, spread, spread, vector),
        check_vma=False,
    )
```

time: 91.5 us -> 69.3 us (0.76)
  Pallas kernels: 74.7 us -> 61.7 us
  local copies, waits for them, and re-layouts: 14.3 us -> 6.6 us
  other arithmetic: 1.33 us -> 0 us
    pallas_call x3 -> x2, Pallas kernels: 74.7 us -> 61.7 us  [the longest x1 59.7 us: on_device(): pl.pallas_call(functools.partial(layer_kernel, regions, subs, tile, k, ch...]
    unnamed x6 -> x2, local copies, waits for them, and re-layouts: 8.5 us -> 3.41 us
    another operation x5 -> x0, local copies, waits for them, and re-layouts: 2.6 us -> none  [the longest x3 1.89 us: on_device(): jnp.stack(ends, axis=1)]
    reshape x2 -> x3, local copies, waits for them, and re-layouts: 1.31 us -> 3.19 us  [on_device(): row = lambda x: x.reshape(1, -1)]
    slice x2 -> x0, local copies, waits for them, and re-layouts: 1.15 us -> none  [on_device(): return (node_grad, edge_grad, gef, ges, mine[0:3], gnf, gns, mine[3:5])]
where the time goes in v2:
time: 69.3 us; the launch traced here: 69 us
  Pallas kernels  61.7 us (89%)
  local copies, waits for them, and re-layouts  6.6 us (10%)
    pallas_call x1, Pallas kernels, on_device(): pl.pallas_call(functools.partial(layer_kernel, regions, subs, tile, k, ch...  59.7 us
    unnamed x2, local copies, waits for them, and re-layouts  3.41 us
    reshape x3, local copies, waits for them, and re-layouts, on_device(): row = lambda x: x.reshape(1, -1)  3.19 us
    pallas_call x1, Pallas kernels, on_device(): pl.pallas_call(split_kernel, out_shape=(shape((nodes, latent), BF16), *(s...  2.01 us

profile of v2, /device:TPU:0, one launch (start us, length us, event | category | flops | bytes accessed | tf_op | source)
XLA Modules:
  0.0 69.0 jit_solution(1029261859432712001)
XLA Ops:
  0.6 1.3 %reshape.41.es_idx = s32[1,1536]{1,0:T(1,128)} reshape(s32[1536]{0:T(1024)} %param.21) | data formatting | bytes 12288 | tf_op jit(solution)/shard_map/reshape | solution.py:481
  1.9 1.3 %reshape.42.er_idx = s32[1,1536]{1,0:T(1,128)} reshape(s32[1536]{0:T(1024)} %param.22) | data formatting | bytes 12288 | tf_op jit(solution)/shard_map/reshape | solution.py:481
  3.2 0.8 %copy.25 = s32[1,16,8]{2,1,0:T(8,128)S(1)} copy(s32[1,16,8]{1,2,0:T(8,128)} %param.20) | data formatting | bytes 1024 | tf_op args[4]
  4.0 0.6 reshape.40.slots_ref
  4.6 59.7 %shard_map.215 = (bf16[1536,512]{1,0:T(8,128)(2,1)}, f32[424,512]{1,0:T(8,128)}) custom-call(bf16[192,512]{1,0:T(8,128)(2,1)} %nl_ref.1, bf16[1536,512]{1,0:T(8,128)(2,1)} %el_ref.1, bf16[192,512]{1,0:T(8,128)(2,1)} %nc_ref.1, bf16[1536,512]{1,0:T(8,128)(2,1)} %ec_ref.1, s32[1,128]{1,0:T(1,128)} %reshape.40.slots_ref, s32[1,1536]{1,0:T(1,128)} %reshape.41.es_idx, ...), custom_call_target="tpu_custom_call" | custom-call | tf_op jit(solution)/shard_map/pallas_call | solution.py:524
  64.3 2.0 %shard_map.216 = (bf16[192,512]{1,0:T(8,128)(2,1)}, f32[32,512]{1,0:T(8,128)}, f32[64,512]{1,0:T(8,128)}, f32[32,512]{1,0:T(8,128)}, f32[96,512]{1,0:T(8,128)}, /*index=5*/f32[3,32]{1,0:T(4,128)}, f32[2,32]{1,0:T(2,128)}) custom-call(f32[424,512]{1,0:T(8,128)} %get-tuple-element.17.small_ref), custom_call_target="tpu_custom_call" | custom-call | tf_op jit(solution)/shard_map/pallas_call | solution.py:552
  66.3 2.7 %copy.27 = bf16[1536,512]{1,0:T(8,128)(2,1)} copy(bf16[1536,512]{1,0:T(8,128)(2,1)} %get-tuple-element.35) | data formatting | bytes 3145728

commit v3 on v2

--- a/solution.py
+++ b/solution.py
@@ -85,25 +85,37 @@
     k,
     chunks,
     nl_ref,
-    el_ref,
+    el_hbm,
     nc_ref,
-    ec_ref,
-    slots_ref,
+    ec_hbm,
+    send_ref,
     es_idx,
     er_idx,
-    ef_ref,
-    es_ref,
+    ef_hbm,
+    es_hbm,
     eb_ref,
     eg_ref,
     esh_ref,
+    nf_hbm,
+    ns_hbm,
+    nb_ref,
+    ng_ref,
+    edge_hbm,
+    small_out,
+    el_ref,
+    ec_ref,
+    ef_ref,
+    es_ref,
     nf_ref,
     ns_ref,
-    nb_ref,
-    ng_ref,
     edge_out,
-    small_out,
+    grad_out_s,
+    grad_pre_s,
+    load_sem,
+    out_sem,
     hot,
     hot_t,
+    rows,
     cols,
     table,
     projected,
@@ -143,8 +155,8 @@
 
     edges, latent = el_ref.shape
     nodes = nl_ref.shape[0]
-    halo = slots_ref.shape[1]
-    slots = halo // peers
+    slots = send_ref.shape[2]
+    halo = peers * slots
     total = 2 * nodes + halo
     edge_scale = 1.0 / math.sqrt(edges * peers)
     node_scale = 1.0 / math.sqrt(nodes * peers)
@@ -156,9 +168,39 @@
     shares = [g.shape[0] // peers for g in grads]
     starts = [sum(shares[:j]) for j in range(5)]
 
+    loads = [
+        pltpu.make_async_copy(source, target, load_sem.at[j])
+        for j, (source, target) in enumerate(
+            (
+                (ef_hbm, ef_ref),
+                (el_hbm, el_ref),
+                (es_hbm, es_ref),
+                (nf_hbm, nf_ref),
+                (ns_hbm, ns_ref),
+                (ec_hbm, ec_ref),
+            )
+        )
+    ]
+
     barrier = greet_all(me, peers, subs)
+    for load in loads:
+        load.start()
     nl = nl_ref[...]
-    slot_col = jnp.transpose(jnp.broadcast_to(slots_ref[...].astype(F32), (8, halo)))[:, 0:1]
+    column = lax.broadcasted_iota(jnp.int32, (slots, halo), 1)
+    repeat = jnp.where(
+        lax.rem(column, slots) == lax.broadcasted_iota(jnp.int32, (slots, halo), 0), 1.0, 0.0
+    )
+    tiled = jnp.dot(
+        send_ref[0].astype(F32),
+        repeat,
+        precision=lax.Precision.HIGHEST,
+        preferred_element_type=F32,
+    )
+    column = lax.broadcasted_iota(jnp.int32, (peers, halo), 1)
+    peer = lax.broadcasted_iota(jnp.int32, (peers, halo), 0) * slots
+    live = (column >= peer) & (column < peer + slots)
+    slot_row = jnp.round(jnp.sum(jnp.where(live, tiled, 0.0), axis=0, keepdims=True))
+    slot_col = jnp.transpose(jnp.broadcast_to(slot_row, (8, halo)))[:, 0:1]
     node_iota = lax.broadcasted_iota(jnp.int32, (halo, nodes), 1).astype(F32)
     picked = mm(one_hot(node_iota == slot_col), nl)
     halo_sent[...] = fold(picked.reshape(peers, slots, latent), 2).astype(BF16)
@@ -180,27 +222,28 @@
 
     halo_got[me] = halo_sent[me]
     table[pl.ds(0, nodes), :] = nl
-    projected[pl.ds(0, nodes), :] = mm(nl, receiver[...]).astype(BF16)
     agg[...] = jnp.zeros_like(agg)
     sums[...] = jnp.zeros_like(sums)
     vec[...] = jnp.zeros_like(vec)
-    cols[...] = jnp.transpose(
-        jnp.concatenate(
-            [
-                jnp.broadcast_to(er_idx[...], (4, edges)),
-                jnp.broadcast_to(es_idx[...] + nodes, (4, edges)),
-            ],
-            axis=0,
-        ).astype(F32)
-    )
+    rows[...] = jnp.concatenate(
+        [
+            jnp.broadcast_to(er_idx[...][None, :], (4, edges)),
+            jnp.broadcast_to(es_idx[...][None, :] + nodes, (4, edges)),
+        ],
+        axis=0,
+    ).astype(F32)
+    cols[...] = jnp.transpose(rows[...])
+    loads[0].wait()
+    projected[pl.ds(0, nodes), :] = mm(nl, receiver[...]).astype(BF16)
+    loads[1].wait()
 
     @pl.loop(0, steps)
     def _(t):
         at = pl.ds(pl.multiple_of(t * tile, tile), tile)
         iota = lax.broadcasted_iota(jnp.int32, (tile, total), 1).astype(F32)
         hot[at, :] = one_hot((cols[at, 0:1] == iota) | (cols[at, 4:5] == iota))
-        iota_t = lax.broadcasted_iota(jnp.int32, (total, tile), 0)
-        hot_t[:, at] = one_hot((er_idx[:, at] == iota_t) | (es_idx[:, at] + nodes == iota_t))
+        iota_t = lax.broadcasted_iota(jnp.int32, (total, tile), 0).astype(F32)
+        hot_t[:, at] = one_hot((rows[0:1, at] == iota_t) | (rows[4:5, at] == iota_t))
         dsilu_s[at, :] = mm(el_ref[at, :], first[...]) + eb_ref[...]
 
     @pl.loop(1, peers)
@@ -211,6 +254,8 @@
         unfold(halo_got[...].astype(F32), 2).reshape(halo, latent).astype(BF16)
     )
     projected[pl.ds(nodes, nodes + halo), :] = mm(table[...], sender[...]).astype(BF16)
+
+    loads[2].wait()
 
     @pl.loop(0, steps)
     def _(t):
@@ -324,6 +369,8 @@
     second_chunks = [c for c, (g, _, _) in enumerate(chunks) if g == 2]
     first_chunks = [c for c, (g, _, _) in enumerate(chunks) if g == 3]
 
+    loads[3].wait()
+    loads[4].wait()
     aggregate = agg[...].astype(BF16)
     top = nf_ref.at[pl.ds(0, latent)]
     low = nf_ref.at[pl.ds(latent, latent)]
@@ -346,6 +393,8 @@
     gef_ref[pl.ds(0, latent), :] = jnp.zeros((latent, latent), F32)
     ges_ref[...] = jnp.zeros_like(ges_ref)
 
+    loads[5].wait()
+
     @pl.loop(0, steps)
     def _(t):
         at = pl.ds(pl.multiple_of(t * tile, tile), tile)
@@ -353,28 +402,33 @@
         grad = cot + mm(hot[at, pl.ds(0, nodes)], projected[pl.ds(0, nodes), :])
         normed = normed_s[at, :]
         grad_out = norm_backward(grad, eg_ref[...], normed, inverse_s[at, :])
-        grad_before = mm_nt(grad_out, es_ref[...]) * dsilu_s[at, :]
-        grad_pre = grad_before.astype(BF16)
-        vec[0:1, :] += jnp.sum(grad_before, axis=0, keepdims=True) * edge_scale
+        grad_out_s[at, :] = grad_out
         vec[1:2, :] += jnp.sum(grad * normed, axis=0, keepdims=True) * edge_scale
         vec[2:3, :] += jnp.sum(grad, axis=0, keepdims=True) * edge_scale
-        edge_out[at, :] = (cot + mm_nt(grad_pre, first[...])).astype(BF16)
+        ges_ref[...] += mm_tn(active_s[at, :], grad_out) * edge_scale
+
+    for c in second_chunks:
+        stage_1(c)
+    for c in node_chunks:
+        stage_2(c)
+
+    @pl.loop(0, steps)
+    def _(t):
+        at = pl.ds(pl.multiple_of(t * tile, tile), tile)
+        grad_before = mm_nt(grad_out_s[at, :], es_ref[...]) * dsilu_s[at, :]
+        grad_pre = grad_before.astype(BF16)
+        grad_pre_s[at, :] = grad_pre
+        vec[0:1, :] += jnp.sum(grad_before, axis=0, keepdims=True) * edge_scale
         sums[...] += mm(hot_t[:, at], grad_pre)
-        ges_ref[...] += mm_tn(active_s[at, :], grad_out) * edge_scale
         gef_ref[pl.ds(0, latent), :] += mm_tn(el_ref[at, :], grad_pre) * edge_scale
-
-        @pl.when(t == 0)
-        def _():
-            for c in node_chunks:
-                stage_2(c)
 
         @pl.when(t == min(1, steps - 1))
         def _():
+            for c in second_chunks:
+                stage_2(c)
             for c in node_chunks:
                 stage_3(c)
 
-    for c in second_chunks:
-        stage_1(c)
     received = sums[pl.ds(0, nodes), :].astype(BF16)
     sent = sums[pl.ds(nodes, nodes + halo), :].astype(BF16)
     gef_ref[pl.ds(latent, latent), :] = mm_tn(table[...], sent) * edge_scale
@@ -389,19 +443,33 @@
         ],
         axis=1,
     ).astype(BF16)
+    for c in first_chunks:
+        stage_2(c)
 
     @pl.loop(1, peers)
     def _(d):
         ret_copy(d, lax.rem(me + d, peers), me).start()
 
     got[me] = ret_ref[me]
-    for c in second_chunks + first_chunks:
-        stage_2(c)
+    for c in second_chunks:
+        stage_3(c)
     node_part[...] += back[:nodes] + mm_nt(received, receiver[...])
-    for c in node_chunks:
+
+    def edge_copy(t):
+        at = pl.ds(pl.multiple_of(t * tile, tile), tile)
+        return pltpu.make_async_copy(edge_out.at[at], edge_hbm.at[at], out_sem.at[t])
+
+    @pl.loop(0, steps)
+    def _(t):
+        at = pl.ds(pl.multiple_of(t * tile, tile), tile)
+        cot = ec_ref[at, :].astype(F32)
+        edge_out[at, :] = (cot + mm_nt(grad_pre_s[at, :], first[...])).astype(BF16)
+        edge_copy(t).start()
+
+    for c in first_chunks:
+        stage_3(c)
+    for c in node_chunks + second_chunks:
         finish(c)
-    for c in second_chunks + first_chunks:
-        stage_3(c)
 
     @pl.loop(1, peers)
     def _(d):
@@ -415,10 +483,16 @@
         mine = jnp.where(me == p, vectors[:, p * width : (p + 1) * width], mine)
     small_out[pl.ds(starts[4], 8), pl.ds(0, width)] = mine
     returned = arrived[:, :slots].reshape(halo, latent).astype(BF16)
-    spread = one_hot(lax.broadcasted_iota(jnp.int32, (nodes, halo), 0) == slots_ref[...])
+    spread = one_hot(
+        lax.broadcasted_iota(jnp.int32, (nodes, halo), 0).astype(F32) == slot_row
+    )
     small_out[pl.ds(starts[4] + 8, nodes), :] = node_part[...] + mm(spread, returned)
-    for c in second_chunks + first_chunks:
+    for c in first_chunks:
         finish(c)
+
+    @pl.loop(0, steps)
+    def _(t):
+        edge_copy(t).wait()
 
     for c in range(len(chunks)):
         copy_1(c).wait_send()
@@ -434,7 +508,19 @@
         ret_copy(d, lax.rem(me + d, peers), me).wait_send()
 
 
-def split_kernel(small_ref, node_out, gns_out, gnf_out, ges_out, gef_out, ev_out, nv_out):
+def split_kernel(
+    small_ref, edge_ref, node_out, gns_out, gnf_out, ges_out, gef_out, ev_out, nv_out, edge_out, sem
+):
+    parts = sem.shape[0]
+    each = edge_ref.shape[0] // parts
+    copies = [
+        pltpu.make_async_copy(
+            edge_ref.at[pl.ds(j * each, each)], edge_out.at[pl.ds(j * each, each)], sem.at[j]
+        )
+        for j in range(parts)
+    ]
+    for copy in copies:
+        copy.start()
     row = 0
     for out in (gns_out, gnf_out, ges_out, gef_out):
         out[...] = small_ref[pl.ds(row, out.shape[0]), :]
@@ -444,6 +530,8 @@
     ev_out[...] = vectors[0:3, :width]
     nv_out[...] = vectors[3:5, :width]
     node_out[...] = small_ref[pl.ds(row + 8, node_out.shape[0]), :].astype(BF16)
+    for copy in copies:
+        copy.wait()
 
 
 def in_vmem(count):
@@ -490,8 +578,20 @@
     sem = pltpu.SemaphoreType.DMA
     count = len(chunks)
     scratch = [
+        pltpu.VMEM((edges, latent), BF16),
+        pltpu.VMEM((edges, latent), BF16),
+        pltpu.VMEM(edge_first.shape, BF16),
+        pltpu.VMEM(edge_second.shape, BF16),
+        pltpu.VMEM(node_first.shape, BF16),
+        pltpu.VMEM(node_second.shape, BF16),
+        pltpu.VMEM((edges, latent), BF16),
+        pltpu.VMEM((edges, latent), BF16),
+        pltpu.VMEM((edges, latent), BF16),
+        sem((6,)),
+        sem((edges // tile,)),
         pltpu.VMEM((edges, total), BF16),
         pltpu.VMEM((total, edges), BF16),
+        pltpu.VMEM((8, edges), F32),
         pltpu.VMEM((edges, 8), F32),
         pltpu.VMEM((nodes + halo, latent), BF16),
         pltpu.VMEM((total, latent), BF16),
@@ -520,12 +620,13 @@
     for g, _, width in chunks:
         for lead in (regions, regions, outer, outer, outer, outer):
             scratch.append(pltpu.VMEM((lead, shares[g] * k, width // k), BF16))
+    in_hbm = pl.BlockSpec(memory_space=pl.ANY)
     small_rows = sum(shares) + 8 + nodes
     edge_grad, small = pl.pallas_call(
         functools.partial(layer_kernel, regions, subs, tile, k, chunks),
         out_shape=(shape((edges, latent), BF16), shape((small_rows, latent), F32)),
-        in_specs=in_vmem(16),
-        out_specs=tuple(in_vmem(2)),
+        in_specs=[in_hbm if j in (1, 3, 7, 8, 12, 13) else in_vmem(1)[0] for j in range(16)],
+        out_specs=(in_hbm, *in_vmem(1)),
         scratch_shapes=scratch,
         compiler_params=pltpu.CompilerParams(
             collective_id=0, has_side_effects=True, vmem_limit_bytes=VMEM_LIMIT
@@ -535,9 +636,9 @@
         edge_latent,
         node_cot,
         edge_cot,
-        row(send_rows),
-        row(edge_sender),
-        row(edge_receiver),
+        send_rows,
+        edge_sender,
+        edge_receiver,
         edge_first,
         edge_second,
         row(edge_bias),
@@ -549,17 +650,20 @@
         row(node_gain),
     )
     width = latent // peers
-    node_grad, gns, gnf, ges, gef, ev, nv = pl.pallas_call(
+    node_grad, gns, gnf, ges, gef, ev, nv, edge_grad = pl.pallas_call(
         split_kernel,
         out_shape=(
             shape((nodes, latent), BF16),
             *(shape((m, latent), F32) for m in shares),
             shape((3, width), F32),
             shape((2, width), F32),
+            shape((edges, latent), BF16),
         ),
-        in_specs=in_vmem(1),
-        out_specs=tuple(in_vmem(7)),
-    )(small)
+        in_specs=[*in_vmem(1), in_hbm],
+        out_specs=(*in_vmem(7), in_hbm),
+        scratch_shapes=[sem((math.gcd(edges // 16, 8),))],
+        compiler_params=pltpu.CompilerParams(vmem_limit_bytes=VMEM_LIMIT),
+    )(small, edge_grad)
     return node_grad, edge_grad, gef, ges, ev, gnf, gns, nv
 
 

time: 69.3 us -> 110 us (1.59)
  Pallas kernels: 61.7 us -> 107 us
  local copies, waits for them, and re-layouts: 6.6 us -> 1.36 us
    pallas_call x1, Pallas kernels: 2.01 us -> 50.8 us  [on_device(): pl.pallas_call(split_kernel, out_shape=(shape((nodes, latent), BF16), *(s...]
    pallas_call x1, Pallas kernels: 59.7 us -> 56.2 us  [on_device(): pl.pallas_call(functools.partial(layer_kernel, regions, subs, tile, k, ch...]
    reshape x3 -> x0, local copies, waits for them, and re-layouts: 3.19 us -> none  [on_device(): row = lambda x: x.reshape(1, -1)]
    unnamed x2 -> x1, local copies, waits for them, and re-layouts: 3.41 us -> 1.36 us
where the time goes in v3:
time: 110 us; the launch traced here: 109 us
  Pallas kernels  107 us (97%)
  local copies, waits for them, and re-layouts  1.36 us (1%)
    pallas_call x1, Pallas kernels, on_device(): pl.pallas_call(functools.partial(layer_kernel, regions, subs, tile, k, ch...  56.2 us
    pallas_call x1, Pallas kernels, on_device(): pl.pallas_call(split_kernel, out_shape=(shape((nodes, latent), BF16), *(s...  50.8 us

profile of v3, /device:TPU:0, one launch (start us, length us, event | category | flops | bytes accessed | tf_op | source)
XLA Modules:
  0.0 109.0 jit_solution(15072156387521623273)
XLA Ops:
  0.6 1.4 %copy.24.send_ref = s32[1,16,8]{2,1,0:T(8,128)} copy(s32[1,16,8]{1,2,0:T(8,128)} %param.20) | data formatting | bytes 1024 | tf_op args[4]
  2.0 56.2 %shard_map.215 = (bf16[1536,512]{1,0:T(8,128)(2,1)}, f32[424,512]{1,0:T(8,128)}) custom-call(bf16[192,512]{1,0:T(8,128)(2,1)} %nl_ref.1, bf16[1536,512]{1,0:T(8,128)(2,1)} %el_hbm.1, bf16[192,512]{1,0:T(8,128)(2,1)} %nc_ref.1, bf16[1536,512]{1,0:T(8,128)(2,1)} %ec_hbm.1, s32[1,16,8]{2,1,0:T(8,128)} %copy.24.send_ref, s32[1536]{0:T(1024)} %es_idx.1, ...), custom_call_target="tpu_custom_call" | custom-call | tf_op jit(solution)/shard_map/pallas_call | solution.py:625
  58.2 50.8 %shard_map.216 = (bf16[192,512]{1,0:T(8,128)(2,1)}, f32[32,512]{1,0:T(8,128)}, f32[64,512]{1,0:T(8,128)}, f32[32,512]{1,0:T(8,128)}, f32[96,512]{1,0:T(8,128)}, ...) custom-call(f32[424,512]{1,0:T(8,128)} %get-tuple-element.18.small_ref, ...), custom_call_target="tpu_custom_call" | custom-call | tf_op jit(solution)/shard_map/pallas_call | solution.py:653

commit v4 on v3

--- a/solution.py
+++ b/solution.py
@@ -155,7 +155,7 @@
 
     edges, latent = el_ref.shape
     nodes = nl_ref.shape[0]
-    slots = send_ref.shape[2]
+    slots = send_ref.shape[1]
     halo = peers * slots
     total = 2 * nodes + halo
     edge_scale = 1.0 / math.sqrt(edges * peers)
@@ -190,9 +190,10 @@
     repeat = jnp.where(
         lax.rem(column, slots) == lax.broadcasted_iota(jnp.int32, (slots, halo), 0), 1.0, 0.0
     )
-    tiled = jnp.dot(
+    tiled = lax.dot_general(
         send_ref[0].astype(F32),
         repeat,
+        (((0,), (0,)), ((), ())),
         precision=lax.Precision.HIGHEST,
         preferred_element_type=F32,
     )
@@ -509,18 +510,36 @@
 
 
 def split_kernel(
-    small_ref, edge_ref, node_out, gns_out, gnf_out, ges_out, gef_out, ev_out, nv_out, edge_out, sem
+    small_ref,
+    edge_ref,
+    node_out,
+    gns_out,
+    gnf_out,
+    ges_out,
+    gef_out,
+    ev_out,
+    nv_out,
+    edge_out,
+    held,
+    in_sem,
+    out_sem,
 ):
-    parts = sem.shape[0]
+    parts = in_sem.shape[0]
     each = edge_ref.shape[0] // parts
-    copies = [
-        pltpu.make_async_copy(
-            edge_ref.at[pl.ds(j * each, each)], edge_out.at[pl.ds(j * each, each)], sem.at[j]
-        )
-        for j in range(parts)
+    pieces = [pl.ds(j * each, each) for j in range(parts)]
+    loads = [
+        pltpu.make_async_copy(edge_ref.at[at], held.at[at], in_sem.at[j])
+        for j, at in enumerate(pieces)
     ]
-    for copy in copies:
-        copy.start()
+    stores = [
+        pltpu.make_async_copy(held.at[at], edge_out.at[at], out_sem.at[j])
+        for j, at in enumerate(pieces)
+    ]
+    for load in loads:
+        load.start()
+    for load, store in zip(loads, stores):
+        load.wait()
+        store.start()
     row = 0
     for out in (gns_out, gnf_out, ges_out, gef_out):
         out[...] = small_ref[pl.ds(row, out.shape[0]), :]
@@ -530,8 +549,8 @@
     ev_out[...] = vectors[0:3, :width]
     nv_out[...] = vectors[3:5, :width]
     node_out[...] = small_ref[pl.ds(row + 8, node_out.shape[0]), :].astype(BF16)
-    for copy in copies:
-        copy.wait()
+    for store in stores:
+        store.wait()
 
 
 def in_vmem(count):
@@ -620,6 +639,7 @@
     for g, _, width in chunks:
         for lead in (regions, regions, outer, outer, outer, outer):
             scratch.append(pltpu.VMEM((lead, shares[g] * k, width // k), BF16))
+    parts = math.gcd(edges // 16, 8)
     in_hbm = pl.BlockSpec(memory_space=pl.ANY)
     small_rows = sum(shares) + 8 + nodes
     edge_grad, small = pl.pallas_call(
@@ -636,7 +656,7 @@
         edge_latent,
         node_cot,
         edge_cot,
-        send_rows,
+        jnp.swapaxes(send_rows, 1, 2),
         edge_sender,
         edge_receiver,
         edge_first,
@@ -661,7 +681,7 @@
         ),
         in_specs=[*in_vmem(1), in_hbm],
         out_specs=(*in_vmem(7), in_hbm),
-        scratch_shapes=[sem((math.gcd(edges // 16, 8),))],
+        scratch_shapes=[pltpu.VMEM((edges, latent), BF16), sem((parts,)), sem((parts,))],
         compiler_params=pltpu.CompilerParams(vmem_limit_bytes=VMEM_LIMIT),
     )(small, edge_grad)
     return node_grad, edge_grad, gef, ges, ev, gnf, gns, nv

time: 110 us -> 61.9 us (0.56)
  Pallas kernels: 107 us -> 60.5 us
  local copies, waits for them, and re-layouts: 1.36 us -> 0 us
    pallas_call x1, Pallas kernels: 50.8 us -> 4.29 us  [on_device(): pl.pallas_call(split_kernel, out_shape=(shape((nodes, latent), BF16), *(s...]
    unnamed x1 -> x0, local copies, waits for them, and re-layouts: 1.36 us -> none
where the time goes in v4:
time: 61.9 us; the launch traced here: 61.1 us
  Pallas kernels  60.5 us (98%)
  between operations  0.65 us (1%)
    pallas_call x1, Pallas kernels, on_device(): pl.pallas_call(functools.partial(layer_kernel, regions, subs, tile, k, ch...  56.2 us
    pallas_call x1, Pallas kernels, on_device(): pl.pallas_call(split_kernel, out_shape=(shape((nodes, latent), BF16), *(s...  4.29 us

profile of v4, /device:TPU:0, one launch (start us, length us, event | category | flops | bytes accessed | tf_op | source)
XLA Modules:
  0.0 61.1 jit_solution(15196093348392386830)
XLA Ops:
  0.6 56.2 %shard_map.215 = (bf16[1536,512]{1,0:T(8,128)(2,1)}, f32[424,512]{1,0:T(8,128)}) custom-call(bf16[192,512]{1,0:T(8,128)(2,1)} %nl_ref.1, bf16[1536,512]{1,0:T(8,128)(2,1)} %el_hbm.1, bf16[192,512]{1,0:T(8,128)(2,1)} %nc_ref.1, bf16[1536,512]{1,0:T(8,128)(2,1)} %ec_hbm.1, s32[1,8,16]{2,1,0:T(8,128)} %bitcast.6, s32[1536]{0:T(1024)} %es_idx.1, s32[1536]{0:T(1024)} %er_idx.1, ...), custom_call_target="tpu_custom_call" | custom-call | tf_op jit(solution)/shard_map/pallas_call | solution.py:645
  56.8 4.3 %shard_map.216 = (bf16[192,512]{1,0:T(8,128)(2,1)}, f32[32,512]{1,0:T(8,128)}, f32[64,512]{1,0:T(8,128)}, f32[32,512]{1,0:T(8,128)}, f32[96,512]{1,0:T(8,128)}, ...) custom-call(f32[424,512]{1,0:T(8,128)} %get-tuple-element.18.small_ref, ...), custom_call_target="tpu_custom_call" | custom-call | tf_op jit(solution)/shard_map/pallas_call | solution.py:673
